TPU v7x, 128 devices: a whole 4x4x4 slice. The times are simulated.
128 devices in a mesh: dp: 16 (over z_lo, y, core), seq: 8 (over z_hi, x).
Axes of the slice: x: 4, y: 4, z: 4 (z_hi: 2, z_lo: 2; z = z_hi * 2 + z_lo), core: 2. Of those that a mesh axis runs over, the one named last changes fastest.
Arguments:
- hidden: bfloat16 [32768, 1536], P(('dp', 'seq')), may hold values from -24 to 24
- masked: int32 [32768], P(('dp', 'seq')), may hold values 0 or 1
- clip_lengths: int32 [16, 3], P('dp'), may hold values from 1 to 1024, 2048 in all within a row
- qkv_weight: bfloat16 [1536, 2304], replicated, may hold values from -0.5 to 0.5
- cotangent: bfloat16 [32768, 768], P(('dp', 'seq')), may hold values from -6 to 6
Outputs:
- attn_out: bfloat16 [32768, 768], P(('dp', 'seq'))
- weight_grad: float32 [1536, 2304], P(('dp', 'seq'))
Inputs may be any that keep to these rules, and one draw needn't show every extreme that they name: Each row of clip_lengths sums to 2048, and its longest clip has exactly 1024 tokens.
All inputs are finite; a program needn't handle non-finite values. No bound on the sum of `masked` on one device may be relied on, other than what follows from the above.
Results may differ from a plain program's by a relative error of at most 0.017.
Values may be sent and summed in bfloat16 or wider, within the bound.
A program may use at most 192 MiB of HBM per device.

v0:
```python
import math

import jax
import jax.numpy as jnp
from jax import lax
from jax.sharding import PartitionSpec as P

HSIZE = 64


neg_fill = -1e30
score_scale = 0.125


def segment_ids(lengths, first_row, row_span):
    clip_ends = jnp.cumsum(lengths)
    position = first_row + jnp.arange(row_span, dtype=jnp.int32)
    return jnp.sum((position[:, None] >= clip_ends[None, :]).astype(jnp.int32), axis=1)


def rms_rows(hidden):
    widened = hidden.astype(jnp.float32)
    scale_rows = lax.rsqrt(jnp.mean(widened * widened, axis=1, keepdims=True) + 1e-06)
    return (widened * scale_rows).astype(jnp.bfloat16)


def shards(hidden, masked, clip_lengths, qkv_weight, cotangent):
    row_count = hidden.shape[0]
    width = qkv_weight.shape[1] // 3
    head_count = width // HSIZE
    seq_count = lax.axis_size("seq")
    group = row_count * seq_count
    block = math.gcd(group, 1024)
    lengths = clip_lengths[0]
    local_seg = segment_ids(lengths, lax.axis_index("seq") * row_count, row_count)
    whole_seg = segment_ids(lengths, 0, group)
    local_low = local_seg[0]
    local_high = local_seg[-1]
    normed = rms_rows(hidden)
    qkv = jnp.dot(normed, qkv_weight, preferred_element_type=jnp.float32).astype(jnp.bfloat16)
    queries = qkv[:, :width]
    keys_own = qkv[:, width : 2 * width]
    values_own = qkv[:, 2 * width :]
    whole_key, whole_value = (
        lax.all_gather(keys_own, "seq", axis=0, tiled=True),
        lax.all_gather(values_own, "seq", axis=0, tiled=True),
    )
    query_heads = queries.reshape(row_count, head_count, HSIZE)
    whole_key_heads = whole_key.reshape(group, head_count, HSIZE)
    whole_value_heads = whole_value.reshape(group, head_count, HSIZE)

    def forward_step(running, blocks):
        key_block, value_block, seg_block = blocks

        def attend(state):
            maxima, totals, weighted = state
            same_clip = (local_seg[:, None] == seg_block[None, :])[None]
            scores = (
                jnp.einsum(
                    "qhd,khd->hqk", query_heads, key_block, preferred_element_type=jnp.float32
                )
                * score_scale
            )
            scores = jnp.where(same_clip, scores, neg_fill)
            new_max = jnp.maximum(maxima, jnp.max(scores, axis=2))
            weights = jnp.where(same_clip, jnp.exp(scores - new_max[:, :, None]), 0.0)
            shrink = jnp.exp(maxima - new_max)
            totals = totals * shrink + jnp.sum(weights, axis=2)
            weighted = weighted * shrink[:, :, None] + jnp.einsum(
                "hqk,khd->hqd",
                weights.astype(jnp.bfloat16),
                value_block,
                preferred_element_type=jnp.float32,
            )
            return (new_max, totals, weighted)

        touching = (seg_block[0] <= local_high) & (seg_block[-1] >= local_low)
        return (lax.cond(touching, attend, lambda state: state, running), None)

    block_count = group // block
    blocks_in = (
        whole_key_heads.reshape(block_count, block, head_count, HSIZE),
        whole_value_heads.reshape(block_count, block, head_count, HSIZE),
        whole_seg.reshape(block_count, block),
    )
    start_state = (
        jnp.full((head_count, row_count), neg_fill, jnp.float32),
        jnp.zeros((head_count, row_count), jnp.float32),
        jnp.zeros((head_count, row_count, HSIZE), jnp.float32),
    )
    (maxima, totals, weighted), unused_out = lax.scan(forward_step, start_state, blocks_in)
    output = (
        (weighted / totals[:, :, None])
        .transpose(1, 0, 2)
        .reshape(row_count, width)
        .astype(jnp.bfloat16)
    )
    upstream = jnp.where(masked[:, None] == 1, cotangent, jnp.zeros_like(cotangent))
    grad_heads = upstream.reshape(row_count, head_count, HSIZE)
    delta = jnp.sum(
        (upstream.astype(jnp.float32) * output.astype(jnp.float32)).reshape(
            row_count, head_count, HSIZE
        ),
        axis=2,
    )
    delta_heads = delta.T

    def block_grads(key_block, value_block, seg_block):
        same_clip = (local_seg[:, None] == seg_block[None, :])[None]
        scores = (
            jnp.einsum("qhd,khd->hqk", query_heads, key_block, preferred_element_type=jnp.float32)
            * score_scale
        )
        probability = (
            jnp.where(same_clip, jnp.exp(scores - maxima[:, :, None]), 0.0) / totals[:, :, None]
        )
        dprob = jnp.einsum(
            "qhd,khd->hqk", grad_heads, value_block, preferred_element_type=jnp.float32
        )
        score_grad = probability * (dprob - delta_heads[:, :, None])
        return (score_grad.astype(jnp.bfloat16), probability.astype(jnp.bfloat16))

    def slice_block(block_index):
        first_row = block_index * block
        key_block = lax.dynamic_slice_in_dim(whole_key_heads, first_row, block, 0)
        value_block = lax.dynamic_slice_in_dim(whole_value_heads, first_row, block, 0)
        seg_block = lax.dynamic_slice_in_dim(whole_seg, first_row, block, 0)
        touching = (seg_block[0] <= local_high) & (seg_block[-1] >= local_low)
        return (first_row, key_block, value_block, seg_block, touching)

    def fill(block_index, buffers):
        first_row, key_block, value_block, seg_block, touching = slice_block(block_index)
        empty = jnp.zeros((head_count, row_count, block), jnp.bfloat16)
        pair = lax.cond(
            touching,
            lambda unused: block_grads(key_block, value_block, seg_block),
            lambda unused: (empty, empty),
            0,
        )
        return (
            lax.dynamic_update_slice_in_dim(buffers[0], pair[0], first_row, 2),
            lax.dynamic_update_slice_in_dim(buffers[1], pair[1], first_row, 2),
        )

    blank = jnp.zeros((head_count, row_count, group), jnp.bfloat16)
    score_grads, probs_all = lax.fori_loop(0, block_count, fill, (blank, blank))
    query_sum = jnp.einsum(
        "hqk,khd->qhd", score_grads, whole_key_heads, preferred_element_type=jnp.float32
    )
    query_grad = (query_sum * score_scale).reshape(row_count, width).astype(jnp.bfloat16)
    key_part = (
        jnp.einsum("hqk,qhd->khd", score_grads, query_heads, preferred_element_type=jnp.float32)
        * score_scale
    )
    value_part = jnp.einsum(
        "hqk,qhd->khd", probs_all, grad_heads, preferred_element_type=jnp.float32
    )
    both_grads = lax.psum_scatter(
        jnp.concatenate(
            [
                key_part.reshape(row_count * lax.axis_size("seq"), width),
                value_part.reshape(row_count * lax.axis_size("seq"), width),
            ],
            axis=1,
        ).astype(jnp.bfloat16),
        "seq",
        scatter_dimension=0,
        tiled=True,
    ).astype(jnp.float32)
    key_grad = both_grads[:, :width].astype(jnp.bfloat16)
    value_grad = both_grads[:, width:].astype(jnp.bfloat16)
    grads_all = jnp.concatenate([query_grad, key_grad, value_grad], axis=1)
    weight_grad = lax.psum_scatter(
        lax.dot_general(
            normed, grads_all, (((0,), (0,)), ((), ())), preferred_element_type=jnp.float32
        ),
        ("dp", "seq"),
        scatter_dimension=0,
        tiled=True,
    )
    return (output, weight_grad)


def solution(mesh):
    in_specs = (
        P(("dp", "seq"), None),
        P(("dp", "seq")),
        P("dp", None),
        P(),
        P(("dp", "seq"), None),
    )
    out_specs = (P(("dp", "seq"), None), P(("dp", "seq"), None))
    return jax.shard_map(shards, mesh=mesh, in_specs=in_specs, out_specs=out_specs, check_vma=False)
```

profile of v0, /device:TPU:0, one launch (start us, length us, event | category | flops | bytes accessed | tf_op | source)
XLA Modules:
  0.0 970.4 jit_solution(4758135792616968466)
XLA Ops:
  9.2 5.4 convolution_convert_fusion
  19.6 61.6 %all-gather.3.cloned.1.call-done = bf16[2048,768]{1,0:T(8,128)(2,1)} async-done(((bf16[256,768]{1,0:T(8,128)(2,1)}), bf16[2048,768]{1,0:T(8,128)(2,1)}) %all-gather.3.cloned.1.call-update) | async-done | bytes 3145744 | tf_op jit(solution)/shard_map/all_gather | solution.py:45
  81.3 3.2 copy.49
  84.5 4.4 reshape_reshape.6
  88.9 4.5 copy.52
  93.4 52.1 %all-gather.5.cloned.1.call-done = bf16[2048,768]{1,0:T(8,128)(2,1)} async-done(((bf16[256,768]{1,0:T(8,128)(2,1)}), bf16[2048,768]{1,0:T(8,128)(2,1)}) %all-gather.5.cloned.1.call-update) | async-done | bytes 3145744 | tf_op jit(solution)/shard_map/all_gather | solution.py:46
  145.6 3.2 copy.51
  148.8 4.0 reshape_reshape.7
  152.8 4.5 copy.53
  158.9 22.8 %while.29 = (s32[]{:T(128)}, f32[12,256]{1,0:T(8,128)S(1)}, f32[12,256]{1,0:T(8,128)}, f32[12,256,64]{1,2,0:T(8,128)}, s32[2,1024]{1,0:T(2,128)}, /*index=5*/s32...) while((s32[]{:T(128)}, f32[12,256]{1,0:T(8,128)S(1)}, ...), condition=%wide.region_9.10_spmd, body=%wide.region_4.9_spmd.sunk | while | flops 846862336 | bytes 63100888 | solution.py:91
  164.0 12.5 %conditional.4 = ((f32[12,256]{1,0:T(8,128)S(1)}, f32[12,256]{1,0:T(8,128)}, f32[12,256,64]{1,2,0:T(8,128)})) conditional(s32[]{:T(128)} %convert_element_type.107, (f32[12,256]{1,0:T(8,128)S(1)}, f32[12,256]{1,0:T(8,128)}, f32[12,256,64]{1,2,0:T(8,128)}) %tuple.93, (s32[256]{0:T(256)}, s32[1,1024]{1,0:T(1,128)}, bf16[2,1024,12,64]{1,3,2,0:T(8,128)(2,1)}, ...), branch_computations={%region_5.5_spmd, %region_6.8_spmd} | conditional | flops 846862336 | bytes 63092400 | solution.py:78
  165.0 3.5 fusion.1
  168.6 3.1 fusion.3
  172.3 3.3 fusion.12
  187.7 5.6 broadcast_in_dim.82
  193.3 5.6 broadcast_in_dim.82.clone
  198.9 49.0 %while.30 = (s32[]{:T(128)}, bf16[12,256,2048]{1,2,0:T(8,128)(2,1)}, bf16[12,256,2048]{1,2,0:T(8,128)(2,1)}, s32[2048]{0:T(1024)}, s32[]{:T(128)}, /*index=5*/s3...) while((s32[]{:T(128)}, ...), condition=%wide.region_14.15_spmd, body=%wide.region_11.14_spmd.sunk | while | flops 830734336 | bytes 69069240 | solution.py:146
  203.3 13.2 %conditional.5 = (bf16[12,256,1024]{1,2,0:T(8,128)(2,1)}, bf16[12,256,1024]{1,2,0:T(8,128)(2,1)}) conditional(s32[]{:T(128)} %convert_element_type.108, () %tuple.98, (s32[256]{0:T(256)}, s32[1024]{0:T(1024)}, bf16[2048,12,64]{0,2,1:T(8,128)(2,1)}, s32[]{:T(128)}, bf16[256,12,64]{0,2,1:T(8,128)(2,1)S(1)}, /*index=5*/f32[12,256]{1,0:T(8,128)S(1)}, ...), branch_computations={%region_12.12_spmd, %region_13.13_spmd} | conditional | flops 830734336 | bytes 43877964 | solution.py:134
  204.2 7.6 fusion.38
  211.8 4.6 fusion.22
  216.4 10.3 %constant_dynamic-update-slice_fusion.3 = (bf16[12,256,2048]{1,2,0:T(8,128)(2,1)}, bf16[12,256,2048]{1,2,0:T(8,128)(2,1)}) fusion(bf16[12,256,2048]{1,2,0:T(8,128)(2,1)} %get-tuple-element.840, bf16[12,256,1024]{1,2,0:T(8,128)(2,1)} %get-tuple-element.764, s32[]{:T(128)} %select_n.58, bf16[12,256,2048]{1,2,0:T(8,128)(2,1)} %get-tuple-element.839, ...), kind=kLoop, calls=%fused_computation.32.clone.1 | loop fusion | bytes 25166336 | tf_op jit(solution)/shard_map/while/body/eval_jaxpr/dynamic_update_slice | solution.py:142
  231.0 6.5 conditional.5
  231.1 3.2 broadcast.91
  234.3 3.3 broadcast.91.clone
  237.6 10.3 %constant_dynamic-update-slice_fusion.3 = (bf16[12,256,2048]{1,2,0:T(8,128)(2,1)}, bf16[12,256,2048]{1,2,0:T(8,128)(2,1)}) fusion(bf16[12,256,2048]{1,2,0:T(8,128)(2,1)} %get-tuple-element.840, bf16[12,256,1024]{1,2,0:T(8,128)(2,1)} %get-tuple-element.764, s32[]{:T(128)} %select_n.58, bf16[12,256,2048]{1,2,0:T(8,128)(2,1)} %get-tuple-element.839, ...), kind=kLoop, calls=%fused_computation.32.clone.1 | loop fusion | bytes 25166336 | tf_op jit(solution)/shard_map/while/body/eval_jaxpr/dynamic_update_slice | solution.py:142
  247.9 8.5 multiply_convert_fusion
  256.4 10.1 %convolution_convert_fusion.1 = bf16[12,64,2048]{2,1,0:T(8,128)(2,1)} fusion(bf16[256,12,64]{0,2,1:T(8,128)(2,1)S(1)} %copy-done.3, bf16[12,256,2048]{1,2,0:T(8,128)(2,1)} %get-tuple-element.460), kind=kOutput, calls=%fused_computation.37 | convolution fusion | flops 806879232 | bytes 16121856 | tf_op jit(solution)/shard_map/hqk,qhd->khd/dot_general | solution.py:155
  266.5 5.6 pad_maximum_fusion
  272.1 6.7 fusion.30
  278.9 109.1 %reduce-scatter.4.cloned.1.call-done = bf16[256,1536]{0,1:T(8,128)(2,1)} async-done(((bf16[2048,1536]{0,1:T(8,128)(2,1)}), bf16[256,1536]{0,1:T(8,128)(2,1)}) %reduce-scatter.4.cloned.1.call-update) | async-done | bytes 786448 | tf_op jit(solution)/shard_map/reduce_scatter | solution.py:158
  388.0 8.7 fusion.31
  396.7 389.2 %fusion = f32[16,2304]{1,0:T(8,128)S(1)} fusion(f32[1536,2304]{1,0:T(8,128)} %fusion.31), kind=kCustom, calls=%all-reduce-scatter | all-reduce-scatter fusion | flops 4718593 | bytes 14303232
  797.7 9.5 collective-permute-start.16
  807.2 9.5 collective-permute-start.17
  816.8 6.6 collective-permute-start.18
  823.4 3.5 collective-permute-start.19
  826.9 3.2 collective-permute-start.2
  832.3 8.6 collective-permute-start.21
  842.2 3.4 collective-permute-start.23
  848.4 5.2 collective-permute-start.25
  853.6 10.8 %collective-permute-start.26 = (f32[16,2304]{1,0:T(8,128)S(1)}, f32[16,2304]{1,0:T(8,128)S(1)}, u32[]{:S(2)}, u32[]{:S(2)}) collective-permute-start(f32[16,2304]{1,0:T(8,128)S(1)} %fusion), channel_id=1, source_target_pairs={{0,27},{1,28},{2,29},{3,30},{4,31},{5,32},{6,33},{7,34},{8,35},{9,... | collective-permute-start | bytes 442376
  868.2 4.1 collective-permute-start.29
  872.4 4.6 collective-permute-start.3
  877.0 4.5 collective-permute-start.30
  881.5 6.1 collective-permute-start.4
  887.6 5.0 collective-permute-start.5
  898.9 5.8 collective-permute-start.9
  907.8 54.5 %concatenate.10 = f32[524,2304]{1,0:T(8,128)} concatenate(f32[12,2304]{1,0:T(8,128)S(1)} %collective-permute-done.31, f32[16,2304]{1,0:T(8,128)} %copy-done.22, f32[16,2304]{1,0:T(8,128)} %copy-done.20, f32[16,2304]{1,0:T(8,128)} %copy-done.19, f32[16,2304]{1,0:T(8,128)} %copy-done.18, f32[16,2304]{1,0:T(8,128)} %copy-done.17, f32[16,2304]{1,0:T(8,128)} %copy-done.16, ...), dimensions={0} | concatenate | bytes 9658368
  (148 shorter events, 59.7 us)
Async XLA Ops:
  7.2 74.1 %all-gather.3.cloned.1.call-start = ((), (), s32[]{:S(2)}) async-start(), calls=%async_computation.1 | async-start | bytes 3538944 | tf_op jit(solution)/shard_map/all_gather | solution.py:45
  9.2 8.2 copy-start.13
  9.2 9.9 %copy-start.26 = (s32[256]{0:T(256)S(1)}, s32[256]{0:T(256)}, u32[]{:S(2)}) copy-start(s32[256]{0:T(256)} %param.14) | copy-start | bytes 3076
  15.5 130.0 %all-gather.5.cloned.1.call-start = ((), (), s32[]{:S(2)}) async-start(), calls=%async_computation.2 | async-start | bytes 3538944 | tf_op jit(solution)/shard_map/all_gather | solution.py:46
  16.3 371.7 %reduce-scatter.4.cloned.1.call-start = ((), (), s32[]{:S(2)}) async-start(), calls=%async_computation.3 | async-start | bytes 7077888 | tf_op jit(solution)/shard_map/reduce_scatter | solution.py:158
  84.5 9.0 copy-start
  247.9 8.5 copy-start.3
  272.1 115.9 %copy-start.25 = (f32[256]{0:T(256)S(1)}, f32[256]{0:T(256)}, u32[]{:S(2)}) copy-start(f32[256]{0:T(256)} %copy-done.24) | copy-start | bytes 3076
  396.7 508.1 %copy-start.5 = (bf16[12,256,64]{1,2,0:T(8,128)(2,1)S(1)}, bf16[12,256,64]{1,2,0:T(8,128)(2,1)}, u32[]{:S(2)}) copy-start(bf16[12,256,64]{1,2,0:T(8,128)(2,1)} %copy-done.4) | copy-start | bytes 1179652
  785.8 7.9 collective-permute-start
  787.2 5.2 collective-permute-start.31
  788.5 6.6 collective-permute-start.1
  789.8 6.6 collective-permute-start.10
  791.1 6.6 collective-permute-start.11
  792.4 14.8 %collective-permute-start.12 = (f32[16,2304]{1,0:T(8,128)S(1)}, f32[16,2304]{1,0:T(8,128)S(1)}, u32[]{:S(2)}, u32[]{:S(2)}) collective-permute-start(f32[16,2304]{1,0:T(8,128)S(1)} %fusion), channel_id=1, source_target_pairs={{0,13},{1,14},{2,15},{3,16},{4,17},{5,18},{6,19},{7,20},{8,21},{9,... | collective-permute-start | bytes 442376
  793.7 23.0 %collective-permute-start.13 = (f32[16,2304]{1,0:T(8,128)S(1)}, f32[16,2304]{1,0:T(8,128)S(1)}, u32[]{:S(2)}, u32[]{:S(2)}) collective-permute-start(f32[16,2304]{1,0:T(8,128)S(1)} %fusion), channel_id=1, source_target_pairs={{0,14},{1,15},{2,16},{3,17},{4,18},{5,19},{6,20},{7,21},{8,22},{9,... | collective-permute-start | bytes 442376
  795.0 28.3 %collective-permute-start.14 = (f32[16,2304]{1,0:T(8,128)S(1)}, f32[16,2304]{1,0:T(8,128)S(1)}, u32[]{:S(2)}, u32[]{:S(2)}) collective-permute-start(f32[16,2304]{1,0:T(8,128)S(1)} %fusion), channel_id=1, source_target_pairs={{0,15},{1,16},{2,17},{3,18},{4,19},{5,20},{6,21},{7,22},{8,23},{9,... | collective-permute-start | bytes 442376
  796.4 30.5 %collective-permute-start.15 = (f32[16,2304]{1,0:T(8,128)S(1)}, f32[16,2304]{1,0:T(8,128)S(1)}, u32[]{:S(2)}, u32[]{:S(2)}) collective-permute-start(f32[16,2304]{1,0:T(8,128)S(1)} %fusion), channel_id=1, source_target_pairs={{0,16},{1,17},{2,18},{3,19},{4,20},{5,21},{6,22},{7,23},{8,24},{9,... | collective-permute-start | bytes 442376
  797.7 32.4 %collective-permute-start.16 = (f32[16,2304]{1,0:T(8,128)S(1)}, f32[16,2304]{1,0:T(8,128)S(1)}, u32[]{:S(2)}, u32[]{:S(2)}) collective-permute-start(f32[16,2304]{1,0:T(8,128)S(1)} %fusion), channel_id=1, source_target_pairs={{0,17},{1,18},{2,19},{3,20},{4,21},{5,22},{6,23},{7,24},{8,25},{9,... | collective-permute-start | bytes 442376
  807.2 25.1 %collective-permute-start.17 = (f32[16,2304]{1,0:T(8,128)S(1)}, f32[16,2304]{1,0:T(8,128)S(1)}, u32[]{:S(2)}, u32[]{:S(2)}) collective-permute-start(f32[16,2304]{1,0:T(8,128)S(1)} %fusion), channel_id=1, source_target_pairs={{0,18},{1,19},{2,20},{3,21},{4,22},{5,23},{6,24},{7,25},{8,26},{9,... | collective-permute-start | bytes 442376
  816.8 24.1 %collective-permute-start.18 = (f32[16,2304]{1,0:T(8,128)S(1)}, f32[16,2304]{1,0:T(8,128)S(1)}, u32[]{:S(2)}, u32[]{:S(2)}) collective-permute-start(f32[16,2304]{1,0:T(8,128)S(1)} %fusion), channel_id=1, source_target_pairs={{0,19},{1,20},{2,21},{3,22},{4,23},{5,24},{6,25},{7,26},{8,27},{9,... | collective-permute-start | bytes 442376
  823.4 18.8 %collective-permute-start.19 = (f32[16,2304]{1,0:T(8,128)S(1)}, f32[16,2304]{1,0:T(8,128)S(1)}, u32[]{:S(2)}, u32[]{:S(2)}) collective-permute-start(f32[16,2304]{1,0:T(8,128)S(1)} %fusion), channel_id=1, source_target_pairs={{0,20},{1,21},{2,22},{3,23},{4,24},{5,25},{6,26},{7,27},{8,28},{9,... | collective-permute-start | bytes 442376
  826.9 18.7 %collective-permute-start.2 = (f32[16,2304]{1,0:T(8,128)S(1)}, f32[16,2304]{1,0:T(8,128)S(1)}, u32[]{:S(2)}, u32[]{:S(2)}) collective-permute-start(f32[16,2304]{1,0:T(8,128)S(1)} %fusion), channel_id=1, source_target_pairs={{0,3},{1,4},{2,5},{3,6},{4,7},{5,8},{6,9},{7,10},{8,11},{9,12},{10... | collective-permute-start | bytes 442376
  830.1 18.3 %collective-permute-start.20 = (f32[16,2304]{1,0:T(8,128)S(1)}, f32[16,2304]{1,0:T(8,128)S(1)}, u32[]{:S(2)}, u32[]{:S(2)}) collective-permute-start(f32[16,2304]{1,0:T(8,128)S(1)} %fusion), channel_id=1, source_target_pairs={{0,21},{1,22},{2,23},{3,24},{4,25},{5,26},{6,27},{7,28},{8,29},{9,... | collective-permute-start | bytes 442376
  832.3 21.3 %collective-permute-start.21 = (f32[16,2304]{1,0:T(8,128)S(1)}, f32[16,2304]{1,0:T(8,128)S(1)}, u32[]{:S(2)}, u32[]{:S(2)}) collective-permute-start(f32[16,2304]{1,0:T(8,128)S(1)} %fusion), channel_id=1, source_target_pairs={{0,22},{1,23},{2,24},{3,25},{4,26},{5,27},{6,28},{7,29},{8,30},{9,... | collective-permute-start | bytes 442376
  840.9 23.5 %collective-permute-start.22 = (f32[16,2304]{1,0:T(8,128)S(1)}, f32[16,2304]{1,0:T(8,128)S(1)}, u32[]{:S(2)}, u32[]{:S(2)}) collective-permute-start(f32[16,2304]{1,0:T(8,128)S(1)} %fusion), channel_id=1, source_target_pairs={{0,23},{1,24},{2,25},{3,26},{4,27},{5,28},{6,29},{7,30},{8,31},{9,... | collective-permute-start | bytes 442376
  842.2 23.5 %collective-permute-start.23 = (f32[16,2304]{1,0:T(8,128)S(1)}, f32[16,2304]{1,0:T(8,128)S(1)}, u32[]{:S(2)}, u32[]{:S(2)}) collective-permute-start(f32[16,2304]{1,0:T(8,128)S(1)} %fusion), channel_id=1, source_target_pairs={{0,24},{1,25},{2,26},{3,27},{4,28},{5,29},{6,30},{7,31},{8,32},{9,... | collective-permute-start | bytes 442376
  845.6 22.6 %collective-permute-start.24 = (f32[16,2304]{1,0:T(8,128)S(1)}, f32[16,2304]{1,0:T(8,128)S(1)}, u32[]{:S(2)}, u32[]{:S(2)}) collective-permute-start(f32[16,2304]{1,0:T(8,128)S(1)} %fusion), channel_id=1, source_target_pairs={{0,25},{1,26},{2,27},{3,28},{4,29},{5,30},{6,31},{7,32},{8,33},{9,... | collective-permute-start | bytes 442376
  848.4 23.9 %collective-permute-start.25 = (f32[16,2304]{1,0:T(8,128)S(1)}, f32[16,2304]{1,0:T(8,128)S(1)}, u32[]{:S(2)}, u32[]{:S(2)}) collective-permute-start(f32[16,2304]{1,0:T(8,128)S(1)} %fusion), channel_id=1, source_target_pairs={{0,26},{1,27},{2,28},{3,29},{4,30},{5,31},{6,32},{7,33},{8,34},{9,... | collective-permute-start | bytes 442376
  853.6 23.3 %collective-permute-start.26 = (f32[16,2304]{1,0:T(8,128)S(1)}, f32[16,2304]{1,0:T(8,128)S(1)}, u32[]{:S(2)}, u32[]{:S(2)}) collective-permute-start(f32[16,2304]{1,0:T(8,128)S(1)} %fusion), channel_id=1, source_target_pairs={{0,27},{1,28},{2,29},{3,30},{4,31},{5,32},{6,33},{7,34},{8,35},{9,... | collective-permute-start | bytes 442376
  864.4 17.1 %collective-permute-start.27 = (f32[16,2304]{1,0:T(8,128)S(1)}, f32[16,2304]{1,0:T(8,128)S(1)}, u32[]{:S(2)}, u32[]{:S(2)}) collective-permute-start(f32[16,2304]{1,0:T(8,128)S(1)} %fusion), channel_id=1, source_target_pairs={{0,28},{1,29},{2,30},{3,31},{4,32},{5,33},{6,34},{7,35},{8,36},{9,... | collective-permute-start | bytes 442376
  865.7 21.8 %collective-permute-start.28 = (f32[16,2304]{1,0:T(8,128)S(1)}, f32[16,2304]{1,0:T(8,128)S(1)}, u32[]{:S(2)}, u32[]{:S(2)}) collective-permute-start(f32[16,2304]{1,0:T(8,128)S(1)} %fusion), channel_id=1, source_target_pairs={{0,29},{1,30},{2,31},{3,32},{4,33},{5,34},{6,35},{7,36},{8,37},{9,... | collective-permute-start | bytes 442376
  868.2 24.3 %collective-permute-start.29 = (f32[16,2304]{1,0:T(8,128)S(1)}, f32[16,2304]{1,0:T(8,128)S(1)}, u32[]{:S(2)}, u32[]{:S(2)}) collective-permute-start(f32[16,2304]{1,0:T(8,128)S(1)} %fusion), channel_id=1, source_target_pairs={{0,30},{1,31},{2,32},{3,33},{4,34},{5,35},{6,36},{7,37},{8,38},{9,... | collective-permute-start | bytes 442376
  872.3 26.5 %copy-start.16 = (f32[16,2304]{1,0:T(8,128)}, f32[16,2304]{1,0:T(8,128)S(1)}, u32[]{:S(2)}) copy-start(f32[16,2304]{1,0:T(8,128)S(1)} %collective-permute-done.25) | copy-start | bytes 442372
  872.4 22.1 %collective-permute-start.3 = (f32[16,2304]{1,0:T(8,128)S(1)}, f32[16,2304]{1,0:T(8,128)S(1)}, u32[]{:S(2)}, u32[]{:S(2)}) collective-permute-start(f32[16,2304]{1,0:T(8,128)S(1)} %fusion), channel_id=1, source_target_pairs={{0,4},{1,5},{2,6},{3,7},{4,8},{5,9},{6,10},{7,11},{8,12},{9,13},{1... | collective-permute-start | bytes 442376
  877.0 27.7 %copy-start.17 = (f32[16,2304]{1,0:T(8,128)}, f32[16,2304]{1,0:T(8,128)S(1)}, u32[]{:S(2)}) copy-start(f32[16,2304]{1,0:T(8,128)S(1)} %collective-permute-done.26) | copy-start | bytes 442372
  877.0 19.5 %collective-permute-start.30 = (f32[16,2304]{1,0:T(8,128)S(1)}, f32[16,2304]{1,0:T(8,128)S(1)}, u32[]{:S(2)}, u32[]{:S(2)}) collective-permute-start(f32[16,2304]{1,0:T(8,128)S(1)} %fusion), channel_id=1, source_target_pairs={{0,31},{1,32},{2,33},{3,34},{4,35},{5,36},{6,37},{7,38},{8,39},{9,... | collective-permute-start | bytes 442376
  881.5 23.2 %copy-start.18 = (f32[16,2304]{1,0:T(8,128)}, f32[16,2304]{1,0:T(8,128)S(1)}, u32[]{:S(2)}) copy-start(f32[16,2304]{1,0:T(8,128)S(1)} %collective-permute-done.27) | copy-start | bytes 442372
  881.5 17.4 %collective-permute-start.4 = (f32[16,2304]{1,0:T(8,128)S(1)}, f32[16,2304]{1,0:T(8,128)S(1)}, u32[]{:S(2)}, u32[]{:S(2)}) collective-permute-start(f32[16,2304]{1,0:T(8,128)S(1)} %fusion), channel_id=1, source_target_pairs={{0,5},{1,6},{2,7},{3,8},{4,9},{5,10},{6,11},{7,12},{8,13},{9,14},{... | collective-permute-start | bytes 442376
  887.6 17.2 %copy-start.19 = (f32[16,2304]{1,0:T(8,128)}, f32[16,2304]{1,0:T(8,128)S(1)}, u32[]{:S(2)}) copy-start(f32[16,2304]{1,0:T(8,128)S(1)} %collective-permute-done.28) | copy-start | bytes 442372
  887.6 18.1 %collective-permute-start.5 = (f32[16,2304]{1,0:T(8,128)S(1)}, f32[16,2304]{1,0:T(8,128)}, u32[]{:S(2)}, u32[]{:S(2)}) collective-permute-start(f32[16,2304]{1,0:T(8,128)S(1)} %fusion), channel_id=1, source_target_pairs={{0,6},{1,7},{2,8},{3,9},{4,10},{5,11},{6,12},{7,13},{8,14},{9,15},... | collective-permute-start | bytes 442376
  892.5 12.2 %copy-start.20 = (f32[16,2304]{1,0:T(8,128)}, f32[16,2304]{1,0:T(8,128)S(1)}, u32[]{:S(2)}) copy-start(f32[16,2304]{1,0:T(8,128)S(1)} %collective-permute-done.29) | copy-start | bytes 442372
  892.5 13.2 %collective-permute-start.6 = (f32[16,2304]{1,0:T(8,128)S(1)}, f32[16,2304]{1,0:T(8,128)}, u32[]{:S(2)}, u32[]{:S(2)}) collective-permute-start(f32[16,2304]{1,0:T(8,128)S(1)} %fusion), channel_id=1, source_target_pairs={{0,7},{1,8},{2,9},{3,10},{4,11},{5,12},{6,13},{7,14},{8,15},{9,16}... | collective-permute-start | bytes 442376
  894.5 10.2 %copy-start.21 = (f32[16,2304]{1,0:T(8,128)}, f32[16,2304]{1,0:T(8,128)S(1)}, u32[]{:S(2)}) copy-start(f32[16,2304]{1,0:T(8,128)S(1)} %collective-permute-done.3) | copy-start | bytes 442372
  894.5 11.2 %collective-permute-start.7 = (f32[16,2304]{1,0:T(8,128)S(1)}, f32[16,2304]{1,0:T(8,128)}, u32[]{:S(2)}, u32[]{:S(2)}) collective-permute-start(f32[16,2304]{1,0:T(8,128)S(1)} %fusion), channel_id=1, source_target_pairs={{0,8},{1,9},{2,10},{3,11},{4,12},{5,13},{6,14},{7,15},{8,16},{9,17... | collective-permute-start | bytes 442376
  896.4 8.3 copy-start.22
  896.4 9.3 collective-permute-start.8
  898.9 8.9 collective-permute-start.9
  (16 other events, 52.9 us)
Sparse Core Ops, SparseCore 0:
  15.7 65.5 all-gather.2
  84.1 61.3 all-gather.4
  272.2 115.7 reduce-scatter.3
where the time goes:
time: 981 us; the launch traced here: 970 us
  blocking collectives  389 us (40%)
  waiting for transfers between devices  226 us (23%)
  local copies, waits for them, and re-layouts  136 us (14%)
  starting transfers between devices  118 us (12%)
  matrix products  58.4 us (6%)
  other arithmetic  18.1 us (2%)
  between operations  14.4 us (1%)
  loops' own time  10.2 us (1%)
    unnamed x1, blocking collectives  389 us
    unnamed x32, starting transfers between devices  118 us
    reduce_scatter x1, waiting for transfers between devices, shards(): lax.psum_scatter(jnp.concatenate([key_part.reshape(row_count * lax.axis_s...  109 us
    all_gather x1, waiting for transfers between devices, shards(): lax.all_gather(keys_own, 'seq', axis=0, tiled=True)  61.6 us
    unnamed x45, local copies, waits for them, and re-layouts  59.4 us
    all_gather x1, waiting for transfers between devices, shards(): lax.all_gather(values_own, 'seq', axis=0, tiled=True)  52.1 us
    dynamic_update_slice x2, local copies, waits for them, and re-layouts, fill(): lax.dynamic_update_slice_in_dim(buffers[1], pair[1], first_row, 2)  20.6 us
  transfers between devices with their start and end apart: 35, of which 4 were waited for; matrix products, arithmetic and copies ran while one was open for 2% of the time, Pallas kernels for 0%

commit v1 on v0

v1 whole, which is shorter than its diff:
```python
import functools

import jax
import jax.numpy as jnp
from jax import lax
from jax.experimental import pallas as pl
from jax.experimental.pallas import tpu as pltpu
from jax.sharding import PartitionSpec as P

MESH = pl.DeviceIdType.MESH
VMEM = pltpu.VMEM
HS = 64
NH = 3
GW = NH * HS
BLK = 256
D = 1536
WIDTH = 768
NEG = -1e30
SCALE = 0.125
LIMIT = 60 * 1024 * 1024


def coords():
    dp = lax.axis_index("dp")
    sq = lax.axis_index("seq")
    core = lax.rem(dp, 2)
    y = lax.rem(dp // 2, 4)
    zl = dp // 8
    x = lax.rem(sq, 4)
    zh = sq // 4
    return x, y, zh, zl, core


def dev(x, y, zh, zl, core):
    return ((zl * 4 + y) * 2 + core, zh * 4 + x)


def mod4(v):
    return lax.rem(v, 4)


def greet(partners):
    barrier = pltpu.get_barrier_semaphore()
    for p in partners:
        pl.semaphore_signal(barrier, inc=1, device_id=p, device_id_type=MESH)
    pl.semaphore_wait(barrier, len(partners))


def dot(a, b):
    return jnp.dot(a, b, preferred_element_type=jnp.float32)


def dot_nt(a, b):
    return lax.dot_general(a, b, (((1,), (1,)), ((), ())), preferred_element_type=jnp.float32)


def project_kernel(
    hidden_ref, mask_ref, cot_ref, w_ref,
    qt_ref, ut_ref, kv_ref, nt_ref,
    land, wbuf, usend, wsem, ssem, rsem, zs, zr, us, ur,
):
    x, y, zh, zl, core = coords()
    right = dev(mod4(x + 1), y, zh, zl, core)
    left = dev(mod4(x + 3), y, zh, zl, core)
    far = dev(mod4(x + 2), y, zh, zl, core)
    zp = dev(x, y, 1 - zh, zl, core)
    lane0 = (3 * x) // 2 * 128
    odd = lax.rem(x, 2) == 1

    wcopies = []
    for j in range(3):
        c = pltpu.make_async_copy(
            w_ref.at[:, pl.ds(pl.multiple_of(WIDTH * j + lane0, 128), 256)], wbuf.at[j], wsem.at[j]
        )
        c.start()
        wcopies.append(c)
    greet([right, left, far, zp])

    half = BLK // 2
    top, bot = pl.ds(0, half), pl.ds(half, half)

    def rcopy(src, dst, i, to):
        return pltpu.make_async_remote_copy(
            src_ref=src, dst_ref=dst, send_sem=ssem.at[i], recv_sem=rsem.at[i],
            device_id=to, device_id_type=MESH,
        )

    a0 = rcopy(hidden_ref.at[top], land.at[0, top], 0, right)
    a1 = rcopy(hidden_ref.at[bot], land.at[1, bot], 1, left)
    a2 = rcopy(hidden_ref.at[bot], land.at[0, bot], 2, right)
    a3 = rcopy(hidden_ref.at[top], land.at[1, top], 3, left)
    for c in (a0, a1, a2, a3):
        c.start()
    b0 = rcopy(land.at[0, top], land.at[2, top], 4, right)
    b1 = rcopy(land.at[1, bot], land.at[2, bot], 5, left)

    upstream = jnp.where(mask_ref[...] == 1, cot_ref[...].astype(jnp.float32), 0.0)
    for g in range(4):
        usend[g] = upstream[:, GW * g : GW * (g + 1)].T.astype(jnp.bfloat16)
    for c in wcopies:
        c.wait()

    def pick(r):
        return jnp.where(odd, r[:, 64:256], r[:, 0:192])

    def process(h, xb):
        h = h.astype(jnp.float32)
        scale = lax.rsqrt(jnp.mean(h * h, axis=1, keepdims=True) + 1e-06)
        normed = (h * scale).astype(jnp.bfloat16)
        q = pick(dot(normed, wbuf[0])).astype(jnp.bfloat16).astype(jnp.float32)
        qt_ref[xb] = (q * SCALE).T.astype(jnp.bfloat16)
        k = pick(dot(normed, wbuf[1]))
        v = pick(dot(normed, wbuf[2]))
        kv_ref[zh * 4 + xb] = jnp.concatenate([k, v], axis=1).astype(jnp.bfloat16)
        c = pltpu.make_async_remote_copy(
            src_ref=kv_ref.at[zh * 4 + xb], dst_ref=kv_ref.at[zh * 4 + xb],
            send_sem=zs.at[xb], recv_sem=zr.at[xb], device_id=zp, device_id_type=MESH,
        )
        c.start()
        nt = normed.T
        lanes = pl.ds(pl.multiple_of(xb * BLK, BLK), BLK)
        for j in range(8):
            for c2 in range(2):
                nt_ref[c2, 96 * j : 96 * (j + 1), lanes] = nt[192 * j + 96 * c2 : 192 * j + 96 * (c2 + 1), :]

    process(hidden_ref[...], x)
    a0.wait_recv()
    b0.start()
    a1.wait_recv()
    b1.start()
    ucopies = []
    for d, to in ((1, right), (2, far), (3, left)):
        c = pltpu.make_async_remote_copy(
            src_ref=usend.at[mod4(x + d)], dst_ref=ut_ref.at[x],
            send_sem=us.at[d - 1], recv_sem=ur.at[d - 1], device_id=to, device_id_type=MESH,
        )
        c.start()
        ucopies.append(c)
    ut_ref[x] = usend[x]
    a2.wait_recv()
    process(land[0], mod4(x + 3))
    a3.wait_recv()
    process(land[1], mod4(x + 1))
    b0.wait_recv()
    b1.wait_recv()
    process(land[2], mod4(x + 2))
    for c in (a0, a1, a2, a3, b0, b1):
        c.wait_send()
    for c in ucopies:
        c.wait()
    for xb in range(4):
        ours, theirs = zh * 4 + xb, (1 - zh) * 4 + xb
        pltpu.make_async_remote_copy(
            src_ref=kv_ref.at[ours], dst_ref=kv_ref.at[ours], send_sem=zs.at[xb], recv_sem=zr.at[xb],
            device_id=zp, device_id_type=MESH,
        ).wait_send()
        pltpu.make_async_remote_copy(
            src_ref=kv_ref.at[theirs], dst_ref=kv_ref.at[theirs], send_sem=zs.at[xb], recv_sem=zr.at[xb],
            device_id=zp, device_id_type=MESH,
        ).wait_recv()


def project(hidden, mask, cot, w):
    bf = jnp.bfloat16
    return pl.pallas_call(
        project_kernel,
        out_shape=(
            jax.ShapeDtypeStruct((4, GW, BLK), bf),
            jax.ShapeDtypeStruct((4, GW, BLK), bf),
            jax.ShapeDtypeStruct((8, BLK, 2 * GW), bf),
            jax.ShapeDtypeStruct((2, WIDTH, 4 * BLK), bf),
        ),
        in_specs=[pl.BlockSpec(memory_space=VMEM)] * 3 + [pl.BlockSpec(memory_space=pl.ANY)],
        out_specs=[pl.BlockSpec(memory_space=VMEM)] * 4,
        scratch_shapes=[
            VMEM((3, BLK, D), bf),
            VMEM((3, D, 256), bf),
            VMEM((4, GW, BLK), bf),
            pltpu.SemaphoreType.DMA((3,)),
            pltpu.SemaphoreType.DMA((6,)),
            pltpu.SemaphoreType.DMA((6,)),
            pltpu.SemaphoreType.DMA((4,)),
            pltpu.SemaphoreType.DMA((4,)),
            pltpu.SemaphoreType.DMA((3,)),
            pltpu.SemaphoreType.DMA((3,)),
        ],
        compiler_params=pltpu.CompilerParams(collective_id=0, has_side_effects=True, vmem_limit_bytes=LIMIT),
        name="project",
    )(hidden, mask, cot, w)


def attend_kernel(
    sc_ref, qt_ref, ut_ref, kv_ref, outt_ref, qg_ref, kvg_ref, s_scr, p_scr, kvt, acc, ot, gt
):
    e0, e1, base = sc_ref[0], sc_ref[1], sc_ref[2]
    CH = 256
    acc[...] = jnp.zeros_like(acc)
    for c in range(8):
        kvt[:, CH * c : CH * (c + 1)] = kv_ref[CH * c : CH * (c + 1), :].T

    def segment(pos):
        return (pos >= e0).astype(jnp.int32) + (pos >= e1).astype(jnp.int32)

    @pl.loop(0, 4)
    def _(i):
        r0 = base + BLK * i
        r1 = r0 + BLK - 1
        low = jnp.where(r0 >= e1, e1, jnp.where(r0 >= e0, e0, 0))
        high = jnp.where(r1 < e0, e0, jnp.where(r1 < e1, e1, 2048))
        c0 = low // CH
        c1 = (high + CH - 1) // CH
        qseg = segment(r0 + lax.broadcasted_iota(jnp.int32, (1, BLK), 1))

        def pass1(c, ms):
            rows = pl.ds(pl.multiple_of(c * CH, CH), CH)
            kseg = segment(c * CH + lax.broadcasted_iota(jnp.int32, (CH, 1), 0))
            same = kseg == qseg
            out = []
            for h in range(NH):
                s = dot(kv_ref[rows, HS * h : HS * (h + 1)], qt_ref[i, HS * h : HS * (h + 1), :])
                s = jnp.where(same, s, NEG)
                s_scr[h, rows, :] = s
                out.append(jnp.maximum(ms[h], jnp.max(s, axis=0, keepdims=True)))
            return tuple(out)

        ms = lax.fori_loop(c0, c1, pass1, tuple(jnp.full((1, BLK), NEG, jnp.float32) for _ in range(NH)))
        ot[...] = jnp.zeros_like(ot)
        gt[...] = jnp.zeros_like(gt)

        def pass2(c, ts):
            rows = pl.ds(pl.multiple_of(c * CH, CH), CH)
            out = []
            for h in range(NH):
                p = jnp.exp(s_scr[h, rows, :] - ms[h])
                out.append(ts[h] + jnp.sum(p, axis=0, keepdims=True))
                pb = p.astype(jnp.bfloat16)
                p_scr[h, rows, :] = pb
                ot[HS * h : HS * (h + 1), :] += dot(kvt[GW + HS * h : GW + HS * (h + 1), rows], pb)
            return tuple(out)

        ts = lax.fori_loop(c0, c1, pass2, tuple(jnp.zeros((1, BLK), jnp.float32) for _ in range(NH)))

        deltas, rts, qrs, urs = [], [], [], []
        for h in range(NH):
            cols = slice(HS * h, HS * (h + 1))
            rt = 1.0 / ts[h]
            o = (ot[cols, :] / ts[h]).astype(jnp.bfloat16)
            outt_ref[i, cols, :] = o
            u = ut_ref[i, cols, :].astype(jnp.float32)
            deltas.append(jnp.sum(u * o.astype(jnp.float32), axis=0, keepdims=True))
            rts.append(rt)
            qrs.append((qt_ref[i, cols, :].astype(jnp.float32) * rt).astype(jnp.bfloat16))
            urs.append((u * rt).astype(jnp.bfloat16))

        def pass3(c, carry):
            rows = pl.ds(pl.multiple_of(c * CH, CH), CH)
            kgs, vgs = [], []
            for h in range(NH):
                cols = slice(HS * h, HS * (h + 1))
                dp = dot(kv_ref[rows, GW + HS * h : GW + HS * (h + 1)], ut_ref[i, cols, :])
                pb = p_scr[h, rows, :]
                ds = (pb.astype(jnp.float32) * (dp - deltas[h])).astype(jnp.bfloat16)
                gt[cols, :] += dot(kvt[cols, rows], ds)
                kgs.append(dot_nt(ds, qrs[h]))
                vgs.append(dot_nt(pb, urs[h]))
            acc[rows, :] += jnp.concatenate(kgs + vgs, axis=1)
            return carry

        lax.fori_loop(c0, c1, pass3, 0)
        g = jnp.concatenate([gt[HS * h : HS * (h + 1), :] * (rts[h] * SCALE) for h in range(NH)], axis=0)
        qg_ref[i] = g.T.astype(jnp.bfloat16)

    kvg_ref[...] = acc[...].astype(jnp.bfloat16)


def attend(scalars, qt, ut, kv):
    bf = jnp.bfloat16
    return pl.pallas_call(
        attend_kernel,
        out_shape=(
            jax.ShapeDtypeStruct((4, GW, BLK), bf),
            jax.ShapeDtypeStruct((4, BLK, GW), bf),
            jax.ShapeDtypeStruct((8 * BLK, 2 * GW), bf),
        ),
        in_specs=[pl.BlockSpec(memory_space=pltpu.SMEM)] + [pl.BlockSpec(memory_space=VMEM)] * 3,
        out_specs=[pl.BlockSpec(memory_space=VMEM)] * 3,
        scratch_shapes=[
            VMEM((NH, 8 * BLK, BLK), jnp.float32),
            VMEM((NH, 8 * BLK, BLK), bf),
            VMEM((2 * GW, 8 * BLK), bf),
            VMEM((8 * BLK, 2 * GW), jnp.float32),
            VMEM((GW, BLK), jnp.float32),
            VMEM((GW, BLK), jnp.float32),
        ],
        compiler_params=pltpu.CompilerParams(vmem_limit_bytes=LIMIT),
        name="attend",
    )(scalars, qt, ut, kv)


def reduce_kernel(
    outt_ref, qg_ref, kvg_ref, nt_ref,
    out_ref, wg_ref,
    zland, oland, s1q, r1q, s1k, r1k, s2q, r2q, s2k, r2k, s3, r3,
    zs, zr, os, orr, cs, cr, qs, qr, ks, kr, xs, xr,
):
    x, y, zh, zl, core = coords()
    z = zh * 2 + zl
    zp = dev(x, y, 1 - zh, zl, core)
    cp = dev(x, y, zh, zl, 1 - core)
    xd = [dev(mod4(x + d), y, zh, zl, core) for d in (1, 2, 3)]
    offsets = [(a, b) for a in range(4) for b in range(4) if (a, b) != (0, 0)]

    def yz(a, b):
        yy, zz = mod4(y + a), mod4(z + b)
        return yy, zz // 2, lax.rem(zz, 2)

    yzd = []
    for a, b in offsets:
        yy, hh, ll = yz(a, b)
        yzd.append((dev(x, yy, hh, ll, core), (ll * 4 + yy) * 2 + hh))
    greet([cp] + xd + [d for d, _ in yzd])

    def rcopy(src, dst, ss, rs, to):
        return pltpu.make_async_remote_copy(
            src_ref=src, dst_ref=dst, send_sem=ss, recv_sem=rs, device_id=to, device_id_type=MESH
        )

    zc = rcopy(kvg_ref.at[1 - zh], zland, zs, zr, zp)
    zc.start()
    oc = []
    for i, d in enumerate((1, 2, 3)):
        c = rcopy(outt_ref.at[mod4(x + d)], oland.at[x], os.at[i], orr.at[i], xd[i])
        c.start()
        oc.append(c)
    oland[x] = outt_ref[x]

    def core_step(g, s1, r1, i):
        s1[...] = dot(nt_ref[1 - core], g).astype(jnp.bfloat16)
        c = rcopy(s1, r1, cs.at[i], cr.at[i], cp)
        c.start()
        return c, dot(nt_ref[core], g)

    def spread(c, mine, r1, s2, r2, ss, rs):
        c.wait()
        both = (mine + r1[...].astype(jnp.float32)).astype(jnp.bfloat16)
        for j in range(16):
            s2[j] = both[48 * j : 48 * (j + 1), :]
        copies = []
        for i, (to, j) in enumerate(yzd):
            c2 = rcopy(s2.at[j], r2.at[i], ss.at[i], rs.at[i], to)
            c2.start()
            copies.append(c2)
        return copies

    me = (zl * 4 + y) * 2 + zh
    cq, mine = core_step(qg_ref[...], s1q, r1q, 0)
    qc = spread(cq, mine, r1q, s2q, r2q, qs, qr)
    for c in oc:
        c.wait()
    for g in range(4):
        out_ref[:, GW * g : GW * (g + 1)] = oland[g].astype(jnp.float32).T.astype(jnp.bfloat16)
    zc.wait()
    g = (kvg_ref[zh].astype(jnp.float32) + zland[...].astype(jnp.float32)).astype(jnp.bfloat16)
    ck, mine = core_step(g, s1k, r1k, 1)
    kc = spread(ck, mine, r1k, s2k, r2k, ks, kr)

    def total(copies, s2, r2):
        t = s2[me].astype(jnp.float32)
        for i, c in enumerate(copies):
            c.wait()
            t = t + r2[i].astype(jnp.float32)
        return t

    tq = total(qc, s2q, r2q)
    tk = total(kc, s2k, r2k)
    for xb in range(4):
        s3[xb, 0:12, 0:GW] = tq[12 * xb : 12 * (xb + 1), :]
        s3[xb, 0:12, 256 : 256 + 2 * GW] = tk[12 * xb : 12 * (xb + 1), :]
    xc = []
    for i, d in enumerate((1, 2, 3)):
        c = rcopy(s3.at[mod4(x + d)], r3.at[x], xs.at[i], xr.at[i], xd[i])
        c.start()
        xc.append(c)
    r3[x] = s3[x]
    for c in xc:
        c.wait()
    for xb in range(4):
        wg_ref[:, GW * xb : GW * (xb + 1)] = r3[xb, 0:12, 0:GW]
        wg_ref[:, WIDTH + GW * xb : WIDTH + GW * (xb + 1)] = r3[xb, 0:12, 256 : 256 + GW]
        wg_ref[:, 2 * WIDTH + GW * xb : 2 * WIDTH + GW * (xb + 1)] = r3[xb, 0:12, 256 + GW : 256 + 2 * GW]


def reduce(outt, qg, kvg, nt):
    bf = jnp.bfloat16
    dma = pltpu.SemaphoreType.DMA
    return pl.pallas_call(
        reduce_kernel,
        out_shape=(
            jax.ShapeDtypeStruct((BLK, WIDTH), bf),
            jax.ShapeDtypeStruct((12, 3 * WIDTH), jnp.float32),
        ),
        in_specs=[pl.BlockSpec(memory_space=VMEM)] * 4,
        out_specs=[pl.BlockSpec(memory_space=VMEM)] * 2,
        scratch_shapes=[
            VMEM((4 * BLK, 2 * GW), bf),
            VMEM((4, GW, BLK), bf),
            VMEM((WIDTH, GW), bf),
            VMEM((WIDTH, GW), bf),
            VMEM((WIDTH, 2 * GW), bf),
            VMEM((WIDTH, 2 * GW), bf),
            VMEM((16, 48, GW), bf),
            VMEM((15, 48, GW), bf),
            VMEM((16, 48, 2 * GW), bf),
            VMEM((15, 48, 2 * GW), bf),
            VMEM((4, 16, 640), jnp.float32),
            VMEM((4, 16, 640), jnp.float32),
            dma, dma, dma((3,)), dma((3,)), dma((2,)), dma((2,)),
            dma((15,)), dma((15,)), dma((15,)), dma((15,)), dma((3,)), dma((3,)),
        ],
        compiler_params=pltpu.CompilerParams(collective_id=1, has_side_effects=True, vmem_limit_bytes=LIMIT),
        name="reduce",
    )(outt, qg, kvg, nt)


def shards(hidden, masked, clip_lengths, qkv_weight, cotangent):
    lengths = clip_lengths[0]
    e0 = lengths[0]
    scalars = jnp.stack([e0, e0 + lengths[1], (lax.axis_index("seq") // 4) * (4 * BLK)])
    qt, ut, kv, nt = project(hidden, masked[:, None], cotangent, qkv_weight)
    outt, qg, kvg = attend(scalars, qt, ut, kv.reshape(8 * BLK, 2 * GW))
    out, wg = reduce(outt, qg.reshape(4 * BLK, GW), kvg.reshape(2, 4 * BLK, 2 * GW), nt)
    return out, wg


def solution(mesh):
    in_specs = (
        P(("dp", "seq"), None),
        P(("dp", "seq")),
        P("dp", None),
        P(),
        P(("dp", "seq"), None),
    )
    out_specs = (P(("dp", "seq"), None), P(("dp", "seq"), None))
    return jax.shard_map(shards, mesh=mesh, in_specs=in_specs, out_specs=out_specs, check_vma=False)
```

time: 981 us -> 134 us (0.14); the launches traced: 970 us -> 134 us
  blocking collectives: 389 us -> 0 us
  waiting for transfers between devices: 226 us -> 0 us
  local copies, waits for them, and re-layouts: 136 us -> 6.13 us
  Pallas kernels: 0 us -> 124 us
  starting transfers between devices: 118 us -> 0 us
  matrix products: 58.4 us -> 0 us
  other arithmetic: 18.1 us -> 1.25 us
  between operations: 14.4 us -> 1.92 us
  loops' own time: 10.2 us -> 0 us
    unnamed x1 -> x0, blocking collectives: 389 us -> none
    pallas_call x0 -> x3, Pallas kernels: none -> 124 us  [the longest x1 50.7 us: reduce(): pl.pallas_call(reduce_kernel, out_shape=(jax.ShapeDtypeStruct((BLK, WIDTH...]
    unnamed x32 -> x0, starting transfers between devices: 118 us -> none
    all_gather x2 -> x0, waiting for transfers between devices: 114 us -> none  [the longest x1 61.6 us: shards(): lax.all_gather(keys_own, 'seq', axis=0, tiled=True)]
    reduce_scatter x1 -> x0, waiting for transfers between devices: 109 us -> none  [shards(): lax.psum_scatter(jnp.concatenate([key_part.reshape(row_count * lax.axis_s...]
    dot_general x9 -> x0, matrix products: 58.4 us -> none  [the longest x1 10.1 us: shards(): jnp.einsum('hqk,qhd->khd', probs_all, grad_heads, preferred_element_type=...]
    unnamed x45 -> x2, local copies, waits for them, and re-layouts: 59.4 us -> 3.35 us
    dynamic_update_slice x2 -> x0, local copies, waits for them, and re-layouts: 20.6 us -> none  [fill(): lax.dynamic_update_slice_in_dim(buffers[1], pair[1], first_row, 2)]
  transfers between devices with their start and end apart: 35 -> 0, of which waited for: 4 -> 0; matrix products, arithmetic and copies ran while one was open for 2% -> 0% of each run, Pallas kernels for 0% -> 0%
where the time goes in v1:
time: 134 us
  Pallas kernels  124 us (93%)
  local copies, waits for them, and re-layouts  6.13 us (5%)
  between operations  1.92 us (1%)
    pallas_call x1, Pallas kernels, reduce(): pl.pallas_call(reduce_kernel, out_shape=(jax.ShapeDtypeStruct((BLK, WIDTH...  50.7 us
    pallas_call x1, Pallas kernels, project(): pl.pallas_call(project_kernel, out_shape=(jax.ShapeDtypeStruct((4, GW, BL...  43.7 us
    pallas_call x1, Pallas kernels, attend(): pl.pallas_call(attend_kernel, out_shape=(jax.ShapeDtypeStruct((4, GW, BLK...  29.9 us
    unnamed x2, local copies, waits for them, and re-layouts  3.35 us

profile of v1, /device:TPU:0, one launch (start us, length us, event | category | flops | bytes accessed | tf_op | source)
XLA Modules:
  0.0 133.6 jit_solution(10102258015802989643)
XLA Ops:
  0.6 1.3 fusion
  3.2 1.2 pad_add_fusion.sc_ref
  4.5 1.5 %copy.7.mask_ref = s32[256,1]{1,0:T(8,128)} copy(s32[256,1]{0,1:T(1,128)} %bitcast.10) | data formatting | bytes 2048 | tf_op jit(solution)/shard_map/broadcast_in_dim | solution.py:429
  5.9 43.7 %project.1 = (bf16[4,192,256]{2,1,0:T(8,128)(2,1)}, bf16[4,192,256]{2,1,0:T(8,128)(2,1)}, bf16[8,256,384]{2,1,0:T(8,128)(2,1)}, bf16[2,768,1024]{2,1,0:T(8,128)(2,1)}) custom-call(bf16[256,1536]{1,0:T(8,128)(2,1)} %hidden_ref.1, s32[256,1]{1,0:T(8,128)} %copy.7.mask_ref, bf16[256,768]{1,0:T(8,128)(2,1)} %cot_ref.1, bf16[1536,2304]{1,0:T(8,128)(2,1)} %w_ref.1), custom_call_target="tpu_custom_call" | custom-call | tf_op jit(solution)/shard_map/project/pallas_call | solution.py:165
  49.6 29.9 %attend.1 = (bf16[4,192,256]{2,1,0:T(8,128)(2,1)}, bf16[4,256,192]{2,1,0:T(8,128)(2,1)}, bf16[2048,384]{1,0:T(8,128)(2,1)}) custom-call(s32[3]{0:T(128)} %pad_add_fusion.sc_ref, bf16[4,192,256]{2,1,0:T(8,128)(2,1)} %get-tuple-element.9.qt_ref, bf16[4,192,256]{2,1,0:T(8,128)(2,1)} %get-tuple-element.10.ut_ref, bf16[2048,384]{1,0:T(8,128)(2,1)} %bitcast.7), custom_call_target="tpu_custom_call" | custom-call | tf_op jit(solution)/shard_map/attend/pallas_call | solution.py:278
  79.6 50.7 %reduce.1 = (bf16[256,768]{1,0:T(8,128)(2,1)}, f32[12,2304]{1,0:T(8,128)}) custom-call(bf16[4,192,256]{2,1,0:T(8,128)(2,1)} %get-tuple-element.12.outt_ref, bf16[1024,192]{1,0:T(8,128)(2,1)} %bitcast.9, bf16[2,1024,384]{2,1,0:T(8,128)(2,1)} %bitcast.8, bf16[2,768,1024]{2,1,0:T(8,128)(2,1)} %get-tuple-element.15.nt_ref), custom_call_target="tpu_custom_call" | custom-call | tf_op jit(solution)/shard_map/reduce/pallas_call | solution.py:396
  130.3 1.8 %copy.10 = bf16[256,768]{1,0:T(8,128)(2,1)} copy(bf16[256,768]{1,0:T(8,128)(2,1)} %get-tuple-element.20) | data formatting | bytes 786432
  132.0 1.6 %copy.11 = f32[12,2304]{1,0:T(8,128)} copy(f32[12,2304]{1,0:T(8,128)} %get-tuple-element.21) | data formatting | bytes 221184

commit v2 on v0

v2 whole, which is shorter than its diff:
```python
import functools

import jax
import jax.numpy as jnp
from jax import lax
from jax.experimental import pallas as pl
from jax.experimental.pallas import tpu as pltpu
from jax.sharding import PartitionSpec as P

MESH = pl.DeviceIdType.MESH
VMEM = pltpu.VMEM
BF = jnp.bfloat16
F32 = jnp.float32
HS = 64
NH = 3
GW = NH * HS
BLK = 256
HALF = 4 * BLK
D = 1536
WIDTH = 768
NEG = -1e30
SCALE = 0.125
LIMIT = 62 * 1024 * 1024
STEPS = (1, 2, 3)


def mod4(v):
    return lax.rem(v, 4)


def dot(a, b):
    return jnp.dot(a, b, preferred_element_type=F32)


def dot_nt(a, b):
    return lax.dot_general(a, b, (((1,), (1,)), ((), ())), preferred_element_type=F32)


def lanes(at, size):
    return pl.ds(pl.multiple_of(at, size), size)


def main_kernel(
    len_ref, hidden_ref, mask_ref, cot_ref, w_ref,
    oland, r3,
    land, wbuf, usend, ut, kv, kvt, qz, uz, nt, s_scr, d_scr, p_scr, g_scr,
    qg, own, zsend, zland, osend, s1, r1, mine, s2, r2, s4, r4, s3,
    wsem, hs, hr, ks, kr, us, ur, zs, zr, osm, orm, cs, cr, ys, yr, vs, vr, xs, xr,
):
    dp = lax.axis_index("dp")
    sq = lax.axis_index("seq")
    core, y, zl = lax.rem(dp, 2), lax.rem(dp // 2, 4), dp // 8
    x, zh = lax.rem(sq, 4), sq // 4
    z = zh * 2 + zl

    def dev(x, y, z, core):
        return ((lax.rem(z, 2) * 4 + y) * 2 + core, (z // 2) * 4 + x)

    xd = [dev(mod4(x + d), y, z, core) for d in STEPS]
    yd = [dev(x, mod4(y + d), z, core) for d in STEPS]
    zd = [dev(x, y, mod4(z + d), core) for d in STEPS]
    cp = dev(x, y, z, 1 - core)
    zp = zd[1]
    right, far, left = xd
    lane0 = (3 * x) // 2 * 128
    odd = lax.rem(x, 2) == 1

    def rcopy(src, dst, ss, rs, to):
        return pltpu.make_async_remote_copy(
            src_ref=src, dst_ref=dst, send_sem=ss, recv_sem=rs, device_id=to, device_id_type=MESH
        )

    wcopies = []
    for j in range(3):
        c = pltpu.make_async_copy(
            w_ref.at[:, pl.ds(pl.multiple_of(WIDTH * j + lane0, 128), 256)], wbuf.at[j], wsem.at[j]
        )
        c.start()
        wcopies.append(c)

    barrier = pltpu.get_barrier_semaphore()
    partners = [cp] + xd + yd + zd
    for p in partners:
        pl.semaphore_signal(barrier, inc=1, device_id=p, device_id_type=MESH)
    pl.semaphore_wait(barrier, len(partners))

    half = BLK // 2
    top, bot = pl.ds(0, half), pl.ds(half, half)
    a0 = rcopy(hidden_ref.at[top], land.at[0, top], hs.at[0], hr.at[0], right)
    a1 = rcopy(hidden_ref.at[bot], land.at[1, bot], hs.at[1], hr.at[1], left)
    a2 = rcopy(hidden_ref.at[bot], land.at[0, bot], hs.at[2], hr.at[2], right)
    a3 = rcopy(hidden_ref.at[top], land.at[1, top], hs.at[3], hr.at[3], left)
    for c in (a0, a1, a2, a3):
        c.start()
    b0 = rcopy(land.at[0, top], land.at[2, top], hs.at[4], hr.at[4], right)
    b1 = rcopy(land.at[1, bot], land.at[2, bot], hs.at[5], hr.at[5], left)

    qz[...] = jnp.zeros_like(qz)
    uz[...] = jnp.zeros_like(uz)
    keep = mask_ref[...] == 1
    for g in range(4):
        u = cot_ref[:, GW * g : GW * (g + 1)].astype(F32).T
        usend[g] = jnp.where(keep, u, 0.0).astype(BF)
    for c in wcopies:
        c.wait()

    def slot(xb):
        return jnp.where(zh == 0, xb, 3 - xb)

    def pick(r):
        return jnp.where(odd, r[:, 64:256], r[:, 0:192])

    def turn(c):
        t = jnp.where(zh == 0, c, 7 - c)
        for h in range(NH):
            kvt[h, :, lanes(t * BLK, BLK)] = kv[c, h].T

    def kvcopy(c, xb):
        return rcopy(kv.at[c], kv.at[c], ks.at[xb], kr.at[xb], zp)

    def process(h, xb):
        h = h.astype(F32)
        scale = lax.rsqrt(jnp.mean(h * h, axis=1, keepdims=True) + 1e-06)
        normed = (h * scale).astype(BF)
        k = pick(dot(normed, wbuf[1]))
        v = pick(dot(normed, wbuf[2]))
        c = zh * 4 + xb
        for i in range(NH):
            cols = slice(HS * i, HS * (i + 1))
            kv[c, i] = jnp.concatenate([k[:, cols], v[:, cols]], axis=1).astype(BF)
        kvcopy(c, xb).start()
        q = (pick(dot(normed, wbuf[0])).astype(BF).astype(F32) * SCALE).T.astype(BF)
        for i in range(NH):
            qz[i, 0:HS, lanes(slot(xb) * BLK, BLK)] = q[HS * i : HS * (i + 1), :]
        turned = normed.T
        for j in range(8):
            for par in range(2):
                at = 192 * j + 96 * par
                nt[par, 96 * j : 96 * (j + 1), lanes(xb * BLK, BLK)] = turned[at : at + 96, :]
        turn(c)

    process(hidden_ref[...], x)
    a0.wait_recv()
    b0.start()
    a1.wait_recv()
    b1.start()
    a2.wait_recv()
    process(land[0], mod4(x + 3))
    a3.wait_recv()
    process(land[1], mod4(x + 1))
    for c in (a0, a1, a2, a3, b0, b1):
        c.wait_send()
    ucopies = []
    for i, d in enumerate(STEPS):
        c = rcopy(usend.at[mod4(x + d)], ut.at[x], us.at[i], ur.at[i], xd[i])
        c.start()
        ucopies.append(c)
    ut[x] = usend[x]
    b0.wait_recv()
    b1.wait_recv()
    process(land[2], mod4(x + 2))
    for xb in range(4):
        theirs = (1 - zh) * 4 + xb
        kvcopy(zh * 4 + xb, xb).wait_send()
        kvcopy(theirs, xb).wait_recv()
        turn(theirs)

    def zcopy(h):
        return rcopy(zsend.at[h], zland.at[h], zs.at[h], zr.at[h], zp)

    def ccopy(h):
        return rcopy(s1.at[h], r1.at[h], cs.at[h], cr.at[h], cp)

    def ycopy(h, i):
        return rcopy(s2.at[h, mod4(y + STEPS[i])], r2.at[h, i], ys.at[h, i], yr.at[h, i], yd[i])

    def vcopy(h, i):
        return rcopy(s4.at[h, mod4(z + STEPS[i])], r4.at[h, i], vs.at[h, i], vr.at[h, i], zd[i])

    def ocopy(h, i):
        rows = pl.ds(pl.multiple_of(h * HS, HS), HS)
        return rcopy(osend.at[h, mod4(x + STEPS[i])], oland.at[x, rows], osm.at[h, i], orm.at[h, i], xd[i])

    def to_core(h):
        zcopy(h).wait()
        g = jnp.concatenate([qg[h], (own[h] + zland[h].astype(F32)).astype(BF)], axis=0)
        s1[h] = dot_nt(nt[1 - core], g).astype(BF)
        ccopy(h).start()
        mine[...] = dot_nt(nt[core], g)

    def to_y(h):
        ccopy(h).wait()
        both = (mine[...] + r1[h].astype(F32)).astype(BF)
        for l in range(2):
            for yy in range(4):
                for u in range(2):
                    row = 384 * l + 96 * yy + 48 * u
                    s2[h, yy, 2 * u + l] = both[row : row + 48, :]
        for i in range(3):
            ycopy(h, i).start()

    def to_z(h):
        t = s2[h, y].astype(F32)
        for i in range(3):
            ycopy(h, i).wait()
            t = t + r2[h, i].astype(F32)
        s4[h] = t.astype(BF)
        for i in range(3):
            vcopy(h, i).start()

    e0 = len_ref[0, 0]
    e1 = e0 + len_ref[0, 1]

    def segment(pos):
        return (pos >= e0).astype(jnp.int32) + (pos >= e1).astype(jnp.int32)

    def key_block(t):
        return jnp.where(zh == 0, t, 7 - t)

    def slots(t):
        return range(max(0, t - 4), 4)

    def qpos(j):
        return zh * HALF + BLK * jnp.where(zh == 0, j, 3 - j)

    qsegs = [segment(qpos(j) + lax.broadcasted_iota(jnp.int32, (1, BLK), 1)) for j in range(4)]

    def at(j):
        return slice(BLK * j, BLK * (j + 1))

    def head(h, carry):
        ms = [jnp.full((1, BLK), NEG, F32) for _ in range(4)]
        for t in range(8):
            c = key_block(t)
            kseg = segment(c * BLK + lax.broadcasted_iota(jnp.int32, (BLK, 1), 0))
            for j in slots(t):
                s = dot(kv[c, h], qz[h, :, at(j)])
                s = jnp.where(kseg == qsegs[j], s, NEG)
                s_scr[at(t), at(j)] = s
                ms[j] = jnp.maximum(ms[j], jnp.max(s, axis=0, keepdims=True))

        @pl.when(h == 0)
        def _():
            for c in ucopies:
                c.wait()
            for xb in range(4):
                for i in range(NH):
                    uz[i, HS : 2 * HS, lanes(slot(xb) * BLK, BLK)] = ut[xb, HS * i : HS * (i + 1), :]

        @pl.when(h > 0)
        def _():
            to_core(h - 1)

        ts = [jnp.zeros((1, BLK), F32) for _ in range(4)]
        for t in range(8):
            c = key_block(t)
            for j in slots(t):
                p = jnp.exp(s_scr[at(t), at(j)] - ms[j])
                ts[j] = ts[j] + jnp.sum(p, axis=0, keepdims=True)
                p_scr[at(t), at(j)] = p.astype(BF)
                d_scr[at(t), at(j)] = dot(kv[c, h], uz[h, :, at(j)])

        @pl.when(h > 0)
        def _():
            to_y(h - 1)

        rts, deltas, qrs, urs = [], [], [], []
        for j in range(4):
            rows = slice(0, BLK * (5 + j))
            o = (dot(kvt[h, HS : 2 * HS, rows], p_scr[rows, at(j)]) / ts[j]).astype(BF)
            osend[h, jnp.where(zh == 0, j, 3 - j)] = o
            u = uz[h, HS : 2 * HS, at(j)].astype(F32)
            rt = 1.0 / ts[j]
            rts.append(rt)
            deltas.append(jnp.sum(u * o.astype(F32), axis=0, keepdims=True))
            qrs.append((qz[h, 0:HS, at(j)].astype(F32) * rt).astype(BF))
            urs.append((u * rt).astype(BF))
        for i in range(3):
            ocopy(h, i).start()
        oland[x, pl.ds(pl.multiple_of(h * HS, HS), HS), :] = osend[h, x]

        for t in (7, 6, 5, 4, 3, 2, 1, 0):
            kg = jnp.zeros((HS, BLK), F32)
            vg = jnp.zeros((HS, BLK), F32)
            for j in slots(t):
                pb = p_scr[at(t), at(j)]
                ds = (pb.astype(F32) * (d_scr[at(t), at(j)] - deltas[j])).astype(BF)
                g_scr[at(t), at(j)] = ds
                kg = kg + dot_nt(qrs[j], ds)
                vg = vg + dot_nt(urs[j], pb)
            both = jnp.concatenate([kg, vg], axis=0)
            if t >= 4:
                zsend[h, :, lanes(jnp.where(zh == 0, t - 4, 7 - t) * BLK, BLK)] = both.astype(BF)
            else:
                own[h, :, lanes(jnp.where(zh == 0, t, 3 - t) * BLK, BLK)] = both
            if t == 4:
                zcopy(h).start()
        for j in range(4):
            rows = slice(0, BLK * (5 + j))
            g = dot(kvt[h, 0:HS, rows], g_scr[rows, at(j)]) * (rts[j] * SCALE)
            qg[h, :, lanes(jnp.where(zh == 0, j, 3 - j) * BLK, BLK)] = g.astype(BF)

        @pl.when(h > 0)
        def _():
            to_z(h - 1)

        return carry

    lax.fori_loop(0, NH, head, 0)
    to_core(NH - 1)
    to_y(NH - 1)
    to_z(NH - 1)

    for h in range(NH):
        t = s4[h, z].astype(F32)
        for i in range(3):
            vcopy(h, i).wait()
            t = t + r4[h, i].astype(F32)
        for xb in range(4):
            s3[xb, 0:12, GW * h : GW * (h + 1)] = t[12 * xb : 12 * (xb + 1), :]
    xc = []
    for i, d in enumerate(STEPS):
        c = rcopy(s3.at[mod4(x + d)], r3.at[x], xs.at[i], xr.at[i], xd[i])
        c.start()
        xc.append(c)
    r3[x] = s3[x]
    for h in range(NH):
        for i in range(3):
            ocopy(h, i).wait()
    for c in xc:
        c.wait()


def main(lengths, hidden, mask, cot, w):
    dma = pltpu.SemaphoreType.DMA
    return pl.pallas_call(
        main_kernel,
        out_shape=(
            jax.ShapeDtypeStruct((4, GW, BLK), BF),
            jax.ShapeDtypeStruct((4, 16, 640), F32),
        ),
        in_specs=[pl.BlockSpec(memory_space=pltpu.SMEM)]
        + [pl.BlockSpec(memory_space=VMEM)] * 3
        + [pl.BlockSpec(memory_space=pl.ANY)],
        out_specs=[pl.BlockSpec(memory_space=VMEM)] * 2,
        scratch_shapes=[
            VMEM((3, BLK, D), BF),
            VMEM((3, D, 256), BF),
            VMEM((4, GW, BLK), BF),
            VMEM((4, GW, BLK), BF),
            VMEM((8, NH, BLK, 2 * HS), BF),
            VMEM((NH, 2 * HS, 8 * BLK), BF),
            VMEM((NH, 2 * HS, HALF), BF),
            VMEM((NH, 2 * HS, HALF), BF),
            VMEM((2, WIDTH, HALF), BF),
            VMEM((8 * BLK, HALF), F32),
            VMEM((8 * BLK, HALF), F32),
            VMEM((8 * BLK, HALF), BF),
            VMEM((8 * BLK, HALF), BF),
            VMEM((NH, HS, HALF), BF),
            VMEM((NH, 2 * HS, HALF), F32),
            VMEM((NH, 2 * HS, HALF), BF),
            VMEM((NH, 2 * HS, HALF), BF),
            VMEM((NH, 4, HS, BLK), BF),
            VMEM((NH, WIDTH, GW), BF),
            VMEM((NH, WIDTH, GW), BF),
            VMEM((WIDTH, GW), F32),
            VMEM((NH, 4, 4, 48, GW), BF),
            VMEM((NH, 3, 4, 48, GW), BF),
            VMEM((NH, 4, 48, GW), BF),
            VMEM((NH, 3, 48, GW), BF),
            VMEM((4, 16, 640), F32),
            dma((3,)), dma((6,)), dma((6,)), dma((4,)), dma((4,)), dma((3,)), dma((3,)),
            dma((NH,)), dma((NH,)), dma((NH, 3)), dma((NH, 3)), dma((NH,)), dma((NH,)),
            dma((NH, 3)), dma((NH, 3)), dma((NH, 3)), dma((NH, 3)), dma((3,)), dma((3,)),
        ],
        compiler_params=pltpu.CompilerParams(collective_id=0, has_side_effects=True, vmem_limit_bytes=LIMIT),
        name="main",
    )(lengths, hidden, mask, cot, w)


def lay_out_kernel(ot_ref, w_ref, out_ref, wg_ref):
    for g in range(4):
        at = GW * g
        out_ref[:, at : at + GW] = ot_ref[g].astype(F32).T.astype(BF)
        for h in range(NH):
            for part in range(3):
                src = GW * h + HS * part
                to = WIDTH * part + at + HS * h
                wg_ref[:, to : to + HS] = w_ref[g, 0:12, src : src + HS]


def lay_out(ot, w):
    return pl.pallas_call(
        lay_out_kernel,
        out_shape=(
            jax.ShapeDtypeStruct((BLK, WIDTH), BF),
            jax.ShapeDtypeStruct((12, 3 * WIDTH), F32),
        ),
        in_specs=[pl.BlockSpec(memory_space=VMEM)] * 2,
        out_specs=[pl.BlockSpec(memory_space=VMEM)] * 2,
        name="lay_out",
    )(ot, w)


def shards(hidden, masked, clip_lengths, qkv_weight, cotangent):
    ot, w = main(clip_lengths, hidden, masked.reshape(1, BLK), cotangent, qkv_weight)
    return lay_out(ot, w)


def solution(mesh):
    in_specs = (
        P(("dp", "seq"), None),
        P(("dp", "seq")),
        P("dp", None),
        P(),
        P(("dp", "seq"), None),
    )
    out_specs = (P(("dp", "seq"), None), P(("dp", "seq"), None))
    return jax.shard_map(shards, mesh=mesh, in_specs=in_specs, out_specs=out_specs, check_vma=False)
```

time: 981 us -> 103 us (0.10); the launches traced: 970 us -> 103 us
  blocking collectives: 389 us -> 0 us
  waiting for transfers between devices: 226 us -> 0 us
  local copies, waits for them, and re-layouts: 136 us -> 0 us
  starting transfers between devices: 118 us -> 0 us
  Pallas kernels: 0 us -> 102 us
  matrix products: 58.4 us -> 0 us
  other arithmetic: 18.1 us -> 0 us
  between operations: 14.4 us -> 0.64 us
  loops' own time: 10.2 us -> 0 us
    unnamed x1 -> x0, blocking collectives: 389 us -> none
    unnamed x32 -> x0, starting transfers between devices: 118 us -> none
    all_gather x2 -> x0, waiting for transfers between devices: 114 us -> none  [the longest x1 61.6 us: shards(): lax.all_gather(keys_own, 'seq', axis=0, tiled=True)]
    reduce_scatter x1 -> x0, waiting for transfers between devices: 109 us -> none  [shards(): lax.psum_scatter(jnp.concatenate([key_part.reshape(row_count * lax.axis_s...]
    pallas_call x0 -> x2, Pallas kernels: none -> 102 us  [the longest x1 100 us: main(): pl.pallas_call(main_kernel, out_shape=(jax.ShapeDtypeStruct((4, GW, BLK),...]
    unnamed x45 -> x0, local copies, waits for them, and re-layouts: 59.4 us -> none
    dot_general x9 -> x0, matrix products: 58.4 us -> none  [the longest x1 10.1 us: shards(): jnp.einsum('hqk,qhd->khd', probs_all, grad_heads, preferred_element_type=...]
    dynamic_update_slice x2 -> x0, local copies, waits for them, and re-layouts: 20.6 us -> none  [fill(): lax.dynamic_update_slice_in_dim(buffers[1], pair[1], first_row, 2)]
  transfers between devices with their start and end apart: 35 -> 0, of which waited for: 4 -> 0; matrix products, arithmetic and copies ran while one was open for 2% -> 0% of each run, Pallas kernels for 0% -> 0%
where the time goes in v2:
time: 103 us
  Pallas kernels  102 us (99%)
    pallas_call x1, Pallas kernels, main(): pl.pallas_call(main_kernel, out_shape=(jax.ShapeDtypeStruct((4, GW, BLK),...  100 us
    pallas_call x1, Pallas kernels, lay_out(): pl.pallas_call(lay_out_kernel, out_shape=(jax.ShapeDtypeStruct((BLK, WIDT...  2.14 us

profile of v2, /device:TPU:0, one launch (start us, length us, event | category | flops | bytes accessed | tf_op | source)
XLA Modules:
  0.0 102.9 jit_solution(8002113010046839322)
XLA Ops:
  0.6 100.2 %main.1 = (bf16[4,192,256]{2,1,0:T(8,128)(2,1)}, f32[4,16,640]{2,1,0:T(8,128)}) custom-call(s32[1,3]{1,0:T(1,128)} %len_ref.1, bf16[256,1536]{1,0:T(8,128)(2,1)} %hidden_ref.1, s32[1,256]{1,0:T(1,128)} %bitcast.1, bf16[256,768]{1,0:T(8,128)(2,1)} %cot_ref.1, bf16[1536,2304]{1,0:T(8,128)(2,1)} %w_ref.1), custom_call_target="tpu_custom_call" | custom-call | tf_op jit(solution)/shard_map/main/pallas_call | solution.py:336
  100.8 2.1 %lay_out.1 = (bf16[256,768]{1,0:T(8,128)(2,1)}, f32[12,2304]{1,0:T(8,128)}) custom-call(bf16[4,192,256]{2,1,0:T(8,128)(2,1)} %get-tuple-element.4.ot_ref, f32[4,16,640]{2,1,0:T(8,128)} %get-tuple-element.5.w_ref), custom_call_target="tpu_custom_call" | custom-call | tf_op jit(solution)/shard_map/lay_out/pallas_call | solution.py:394

commit v3 on v2

--- a/solution.py
+++ b/solution.py
@@ -44,8 +44,8 @@
     len_ref, hidden_ref, mask_ref, cot_ref, w_ref,
     oland, r3,
     land, wbuf, usend, ut, kv, kvt, qz, uz, nt, s_scr, d_scr, p_scr, g_scr,
-    qg, own, zsend, zland, osend, s1, r1, mine, s2, r2, s4, r4, s3,
-    wsem, hs, hr, ks, kr, us, ur, zs, zr, osm, orm, cs, cr, ys, yr, vs, vr, xs, xr,
+    qg, own, zsend, zland, osend, s1, r1, mine, s2, r2, s4, r4, s5, r5, s3, nbuf, mx,
+    wsem, hs, hr, ks, kr, us, ur, zs, zr, osm, orm, cs, cr, ys, yr, vs, vr, ds, dr, xs, xr,
 ):
     dp = lax.axis_index("dp")
     sq = lax.axis_index("seq")
@@ -60,6 +60,12 @@
     yd = [dev(x, mod4(y + d), z, core) for d in STEPS]
     zd = [dev(x, y, mod4(z + d), core) for d in STEPS]
     cp = dev(x, y, z, 1 - core)
+    yzd = []
+    for a in range(4):
+        for b in range(4):
+            if (a, b) != (0, 0):
+                yy, zz = mod4(y + a), mod4(z + b)
+                yzd.append((dev(x, yy, zz, core), yy * 4 + zz))
     zp = zd[1]
     right, far, left = xd
     lane0 = (3 * x) // 2 * 128
@@ -79,7 +85,7 @@
         wcopies.append(c)
 
     barrier = pltpu.get_barrier_semaphore()
-    partners = [cp] + xd + yd + zd
+    partners = [cp] + xd + [to for to, _ in yzd]
     for p in partners:
         pl.semaphore_signal(barrier, inc=1, device_id=p, device_id_type=MESH)
     pl.semaphore_wait(barrier, len(partners))
@@ -122,6 +128,7 @@
         h = h.astype(F32)
         scale = lax.rsqrt(jnp.mean(h * h, axis=1, keepdims=True) + 1e-06)
         normed = (h * scale).astype(BF)
+        nbuf[...] = normed
         k = pick(dot(normed, wbuf[1]))
         v = pick(dot(normed, wbuf[2]))
         c = zh * 4 + xb
@@ -129,6 +136,9 @@
             cols = slice(HS * i, HS * (i + 1))
             kv[c, i] = jnp.concatenate([k[:, cols], v[:, cols]], axis=1).astype(BF)
         kvcopy(c, xb).start()
+
+    def finish(xb):
+        normed = nbuf[...]
         q = (pick(dot(normed, wbuf[0])).astype(BF).astype(F32) * SCALE).T.astype(BF)
         for i in range(NH):
             qz[i, 0:HS, lanes(slot(xb) * BLK, BLK)] = q[HS * i : HS * (i + 1), :]
@@ -137,17 +147,26 @@
             for par in range(2):
                 at = 192 * j + 96 * par
                 nt[par, 96 * j : 96 * (j + 1), lanes(xb * BLK, BLK)] = turned[at : at + 96, :]
-        turn(c)
+        turn(zh * 4 + xb)
+
+    def arrive(xb):
+        theirs = (1 - zh) * 4 + xb
+        kvcopy(theirs, xb).wait_recv()
+        turn(theirs)
 
     process(hidden_ref[...], x)
     a0.wait_recv()
     b0.start()
     a1.wait_recv()
     b1.start()
+    finish(x)
     a2.wait_recv()
     process(land[0], mod4(x + 3))
+    finish(mod4(x + 3))
     a3.wait_recv()
     process(land[1], mod4(x + 1))
+    finish(mod4(x + 1))
+    arrive(x)
     for c in (a0, a1, a2, a3, b0, b1):
         c.wait_send()
     ucopies = []
@@ -159,14 +178,10 @@
     b0.wait_recv()
     b1.wait_recv()
     process(land[2], mod4(x + 2))
-    for xb in range(4):
-        theirs = (1 - zh) * 4 + xb
-        kvcopy(zh * 4 + xb, xb).wait_send()
-        kvcopy(theirs, xb).wait_recv()
-        turn(theirs)
-
-    def zcopy(h):
-        return rcopy(zsend.at[h], zland.at[h], zs.at[h], zr.at[h], zp)
+    finish(mod4(x + 2))
+
+    def zcopy(h, part):
+        return rcopy(zsend.at[h, part], zland.at[h, part], zs.at[h, part], zr.at[h, part], zp)
 
     def ccopy(h):
         return rcopy(s1.at[h], r1.at[h], cs.at[h], cr.at[h], cp)
@@ -182,8 +197,11 @@
         return rcopy(osend.at[h, mod4(x + STEPS[i])], oland.at[x, rows], osm.at[h, i], orm.at[h, i], xd[i])
 
     def to_core(h):
-        zcopy(h).wait()
-        g = jnp.concatenate([qg[h], (own[h] + zland[h].astype(F32)).astype(BF)], axis=0)
+        parts = [qg[h]]
+        for part in range(2):
+            zcopy(h, part).wait()
+            parts.append((own[h, part] + zland[h, part].astype(F32)).astype(BF))
+        g = jnp.concatenate(parts, axis=0)
         s1[h] = dot_nt(nt[1 - core], g).astype(BF)
         ccopy(h).start()
         mine[...] = dot_nt(nt[core], g)
@@ -208,6 +226,21 @@
         for i in range(3):
             vcopy(h, i).start()
 
+    def dcopy(i):
+        to, place = yzd[i]
+        return rcopy(s5.at[place], r5.at[i], ds.at[i], dr.at[i], to)
+
+    def to_yz(h):
+        ccopy(h).wait()
+        both = (mine[...] + r1[h].astype(F32)).astype(BF)
+        for l in range(2):
+            for yy in range(4):
+                for u in range(2):
+                    row = 384 * l + 96 * yy + 48 * u
+                    s5[yy * 4 + 2 * u + l] = both[row : row + 48, :]
+        for i in range(15):
+            dcopy(i).start()
+
     e0 = len_ref[0, 0]
     e1 = e0 + len_ref[0, 1]
 
@@ -228,16 +261,19 @@
     def at(j):
         return slice(BLK * j, BLK * (j + 1))
 
-    def head(h, carry):
-        ms = [jnp.full((1, BLK), NEG, F32) for _ in range(4)]
-        for t in range(8):
+    def scores(h, steps):
+        for t in steps:
             c = key_block(t)
             kseg = segment(c * BLK + lax.broadcasted_iota(jnp.int32, (BLK, 1), 0))
             for j in slots(t):
                 s = dot(kv[c, h], qz[h, :, at(j)])
                 s = jnp.where(kseg == qsegs[j], s, NEG)
                 s_scr[at(t), at(j)] = s
-                ms[j] = jnp.maximum(ms[j], jnp.max(s, axis=0, keepdims=True))
+                m = jnp.max(s, axis=0, keepdims=True)
+                mx[0:1, at(j)] = m if t == 0 else jnp.maximum(mx[0:1, at(j)], m)
+
+    def head(h, carry):
+        scores(h, range(4, 8))
 
         @pl.when(h == 0)
         def _():
@@ -247,10 +283,7 @@
                 for i in range(NH):
                     uz[i, HS : 2 * HS, lanes(slot(xb) * BLK, BLK)] = ut[xb, HS * i : HS * (i + 1), :]
 
-        @pl.when(h > 0)
-        def _():
-            to_core(h - 1)
-
+        ms = [mx[0:1, at(j)] for j in range(4)]
         ts = [jnp.zeros((1, BLK), F32) for _ in range(4)]
         for t in range(8):
             c = key_block(t)
@@ -260,41 +293,61 @@
                 p_scr[at(t), at(j)] = p.astype(BF)
                 d_scr[at(t), at(j)] = dot(kv[c, h], uz[h, :, at(j)])
 
-        @pl.when(h > 0)
-        def _():
-            to_y(h - 1)
-
-        rts, deltas, qrs, urs = [], [], [], []
+        rts = [1.0 / ts[j] for j in range(4)]
+        us_ = [uz[h, HS : 2 * HS, at(j)].astype(F32) for j in range(4)]
+        urs = [(us_[j] * rts[j]).astype(BF) for j in range(4)]
+        qrs = [(qz[h, 0:HS, at(j)].astype(F32) * rts[j]).astype(BF) for j in range(4)]
+
+        def put(t, part, g):
+            if t >= 4:
+                zsend[h, part, :, lanes(jnp.where(zh == 0, t - 4, 7 - t) * BLK, BLK)] = g.astype(BF)
+            else:
+                own[h, part, :, lanes(jnp.where(zh == 0, t, 3 - t) * BLK, BLK)] = g
+
+        def value_grad(t):
+            g = jnp.zeros((HS, BLK), F32)
+            for j in slots(t):
+                g = g + dot_nt(urs[j], p_scr[at(t), at(j)])
+            put(t, 1, g)
+
+        def key_grad(t):
+            g = jnp.zeros((HS, BLK), F32)
+            for j in slots(t):
+                ds_ = p_scr[at(t), at(j)].astype(F32) * (d_scr[at(t), at(j)] - deltas[j])
+                ds_ = ds_.astype(BF)
+                g_scr[at(t), at(j)] = ds_
+                g = g + dot_nt(qrs[j], ds_)
+            put(t, 0, g)
+
+        for t in (7, 6, 5, 4):
+            value_grad(t)
+        zcopy(h, 1).start()
+
+        deltas = []
         for j in range(4):
             rows = slice(0, BLK * (5 + j))
             o = (dot(kvt[h, HS : 2 * HS, rows], p_scr[rows, at(j)]) / ts[j]).astype(BF)
             osend[h, jnp.where(zh == 0, j, 3 - j)] = o
-            u = uz[h, HS : 2 * HS, at(j)].astype(F32)
-            rt = 1.0 / ts[j]
-            rts.append(rt)
-            deltas.append(jnp.sum(u * o.astype(F32), axis=0, keepdims=True))
-            qrs.append((qz[h, 0:HS, at(j)].astype(F32) * rt).astype(BF))
-            urs.append((u * rt).astype(BF))
+            deltas.append(jnp.sum(us_[j] * o.astype(F32), axis=0, keepdims=True))
         for i in range(3):
             ocopy(h, i).start()
         oland[x, pl.ds(pl.multiple_of(h * HS, HS), HS), :] = osend[h, x]
 
-        for t in (7, 6, 5, 4, 3, 2, 1, 0):
-            kg = jnp.zeros((HS, BLK), F32)
-            vg = jnp.zeros((HS, BLK), F32)
-            for j in slots(t):
-                pb = p_scr[at(t), at(j)]
-                ds = (pb.astype(F32) * (d_scr[at(t), at(j)] - deltas[j])).astype(BF)
-                g_scr[at(t), at(j)] = ds
-                kg = kg + dot_nt(qrs[j], ds)
-                vg = vg + dot_nt(urs[j], pb)
-            both = jnp.concatenate([kg, vg], axis=0)
-            if t >= 4:
-                zsend[h, :, lanes(jnp.where(zh == 0, t - 4, 7 - t) * BLK, BLK)] = both.astype(BF)
-            else:
-                own[h, :, lanes(jnp.where(zh == 0, t, 3 - t) * BLK, BLK)] = both
-            if t == 4:
-                zcopy(h).start()
+        for t in (7, 6, 5, 4):
+            key_grad(t)
+        zcopy(h, 0).start()
+
+        @pl.when(h == 2)
+        def _():
+            to_z(0)
+
+        @pl.when(h > 0)
+        def _():
+            to_core(h - 1)
+
+        for t in (3, 2, 1, 0):
+            value_grad(t)
+            key_grad(t)
         for j in range(4):
             rows = slice(0, BLK * (5 + j))
             g = dot(kvt[h, 0:HS, rows], g_scr[rows, at(j)]) * (rts[j] * SCALE)
@@ -302,20 +355,35 @@
 
         @pl.when(h > 0)
         def _():
-            to_z(h - 1)
+            to_y(h - 1)
+
+        @pl.when(h < NH - 1)
+        def _():
+            scores(h + 1, range(4))
 
         return carry
 
+    scores(0, range(4))
+    for d in (3, 1, 2):
+        arrive(mod4(x + d))
+    for xb in range(4):
+        kvcopy(zh * 4 + xb, xb).wait_send()
     lax.fori_loop(0, NH, head, 0)
     to_core(NH - 1)
-    to_y(NH - 1)
-    to_z(NH - 1)
+    to_z(1)
+    to_yz(NH - 1)
 
     for h in range(NH):
-        t = s4[h, z].astype(F32)
-        for i in range(3):
-            vcopy(h, i).wait()
-            t = t + r4[h, i].astype(F32)
+        if h < NH - 1:
+            t = s4[h, z].astype(F32)
+            for i in range(3):
+                vcopy(h, i).wait()
+                t = t + r4[h, i].astype(F32)
+        else:
+            t = s5[y * 4 + z].astype(F32)
+            for i in range(15):
+                dcopy(i).wait()
+                t = t + r5[i].astype(F32)
         for xb in range(4):
             s3[xb, 0:12, GW * h : GW * (h + 1)] = t[12 * xb : 12 * (xb + 1), :]
     xc = []
@@ -358,21 +426,26 @@
             VMEM((8 * BLK, HALF), BF),
             VMEM((8 * BLK, HALF), BF),
             VMEM((NH, HS, HALF), BF),
-            VMEM((NH, 2 * HS, HALF), F32),
-            VMEM((NH, 2 * HS, HALF), BF),
-            VMEM((NH, 2 * HS, HALF), BF),
+            VMEM((NH, 2, HS, HALF), F32),
+            VMEM((NH, 2, HS, HALF), BF),
+            VMEM((NH, 2, HS, HALF), BF),
             VMEM((NH, 4, HS, BLK), BF),
             VMEM((NH, WIDTH, GW), BF),
             VMEM((NH, WIDTH, GW), BF),
             VMEM((WIDTH, GW), F32),
-            VMEM((NH, 4, 4, 48, GW), BF),
-            VMEM((NH, 3, 4, 48, GW), BF),
-            VMEM((NH, 4, 48, GW), BF),
-            VMEM((NH, 3, 48, GW), BF),
+            VMEM((NH - 1, 4, 4, 48, GW), BF),
+            VMEM((NH - 1, 3, 4, 48, GW), BF),
+            VMEM((NH - 1, 4, 48, GW), BF),
+            VMEM((NH - 1, 3, 48, GW), BF),
+            VMEM((16, 48, GW), BF),
+            VMEM((15, 48, GW), BF),
             VMEM((4, 16, 640), F32),
+            VMEM((BLK, D), BF),
+            VMEM((8, HALF), F32),
             dma((3,)), dma((6,)), dma((6,)), dma((4,)), dma((4,)), dma((3,)), dma((3,)),
-            dma((NH,)), dma((NH,)), dma((NH, 3)), dma((NH, 3)), dma((NH,)), dma((NH,)),
-            dma((NH, 3)), dma((NH, 3)), dma((NH, 3)), dma((NH, 3)), dma((3,)), dma((3,)),
+            dma((NH, 2)), dma((NH, 2)), dma((NH, 3)), dma((NH, 3)), dma((NH,)), dma((NH,)),
+            dma((NH - 1, 3)), dma((NH - 1, 3)), dma((NH - 1, 3)), dma((NH - 1, 3)), dma((15,)), dma((15,)),
+            dma((3,)), dma((3,)),
         ],
         compiler_params=pltpu.CompilerParams(collective_id=0, has_side_effects=True, vmem_limit_bytes=LIMIT),
         name="main",

time: 103 us -> 90.4 us (0.88)
  Pallas kernels: 102 us -> 89.6 us
    pallas_call x1, Pallas kernels: 100 us -> 87.5 us  [main(): pl.pallas_call(main_kernel, out_shape=(jax.ShapeDtypeStruct((4, GW, BLK),...]
where the time goes in v3:
time: 90.4 us; the launch traced here: 90.3 us
  Pallas kernels  89.6 us (99%)
    pallas_call x1, Pallas kernels, main(): pl.pallas_call(main_kernel, out_shape=(jax.ShapeDtypeStruct((4, GW, BLK),...  87.5 us
    pallas_call x1, Pallas kernels, lay_out(): pl.pallas_call(lay_out_kernel, out_shape=(jax.ShapeDtypeStruct((BLK, WIDT...  2.14 us

profile of v3, /device:TPU:0, one launch (start us, length us, event | category | flops | bytes accessed | tf_op | source)
XLA Modules:
  0.0 90.3 jit_solution(6820430748238153793)
XLA Ops:
  0.6 87.5 %main.1 = (bf16[4,192,256]{2,1,0:T(8,128)(2,1)}, f32[4,16,640]{2,1,0:T(8,128)}) custom-call(s32[1,3]{1,0:T(1,128)} %len_ref.1, bf16[256,1536]{1,0:T(8,128)(2,1)} %hidden_ref.1, s32[1,256]{1,0:T(1,128)} %bitcast.1, bf16[256,768]{1,0:T(8,128)(2,1)} %cot_ref.1, bf16[1536,2304]{1,0:T(8,128)(2,1)} %w_ref.1), custom_call_target="tpu_custom_call" | custom-call | tf_op jit(solution)/shard_map/main/pallas_call | solution.py:404
  88.1 2.1 %lay_out.1 = (bf16[256,768]{1,0:T(8,128)(2,1)}, f32[12,2304]{1,0:T(8,128)}) custom-call(bf16[4,192,256]{2,1,0:T(8,128)(2,1)} %get-tuple-element.4.ot_ref, f32[4,16,640]{2,1,0:T(8,128)} %get-tuple-element.5.w_ref), custom_call_target="tpu_custom_call" | custom-call | tf_op jit(solution)/shard_map/lay_out/pallas_call | solution.py:467

commit v4 on v3

v4 whole, which is shorter than its diff:
```python
import functools

import jax
import jax.numpy as jnp
from jax import lax
from jax.experimental import pallas as pl
from jax.experimental.pallas import tpu as pltpu
from jax.sharding import PartitionSpec as P

MESH = pl.DeviceIdType.MESH
VMEM = pltpu.VMEM
BF = jnp.bfloat16
F32 = jnp.float32
HS = 64
NH = 3
GW = NH * HS
BLK = 256
HALF = 4 * BLK
D = 1536
WIDTH = 768
NEG = -1e30
SCALE = 0.125
LIMIT = 62 * 1024 * 1024
STEPS = (1, 2, 3)


def mod4(v):
    return lax.rem(v, 4)


def dot(a, b):
    return jnp.dot(a, b, preferred_element_type=F32)


def dot_nt(a, b):
    return lax.dot_general(a, b, (((1,), (1,)), ((), ())), preferred_element_type=F32)


def lanes(at, size):
    return pl.ds(pl.multiple_of(at, size), size)


def main_kernel(
    len_ref, hidden_ref, mask_ref, cot_ref, w_ref,
    oland, r3a, r3b,
    land, wbuf, usend, ut, kvsend, kv, kvt, qsend, qland, qz, uz, nt, s_scr, p_scr, g_scr,
    qg, own, zsend, zland, osend, gbuf, theirs, mine, s1a, r1a, s1b, r1b, s5a, r5a, s5b, r5b, s3a, s3b, mx,
    wsem, hs, hr, as_, ar, ps, pr, ks, kr, us, ur, zs, zr, osm, orm, cs, cr, ds, dr, xs, xr,
):
    dp = lax.axis_index("dp")
    sq = lax.axis_index("seq")
    core, y, zl = lax.rem(dp, 2), lax.rem(dp // 2, 4), dp // 8
    x, zh = lax.rem(sq, 4), sq // 4
    z = zh * 2 + zl

    def dev(x, y, z, core):
        return ((lax.rem(z, 2) * 4 + y) * 2 + core, (z // 2) * 4 + x)

    xd = [dev(mod4(x + d), y, z, core) for d in STEPS]
    yd = [dev(x, mod4(y + d), z, core) for d in STEPS]
    zd = [dev(x, y, mod4(z + d), core) for d in STEPS]
    cp = dev(x, y, z, 1 - core)
    yzd = []
    for a in range(4):
        for b in range(4):
            if (a, b) != (0, 0):
                yy, zz = mod4(y + a), mod4(z + b)
                yzd.append((dev(x, yy, zz, core), yy * 4 + zz))
    zp = zd[1]
    right, far, left = xd
    def rcopy(src, dst, ss, rs, to):
        return pltpu.make_async_remote_copy(
            src_ref=src, dst_ref=dst, send_sem=ss, recv_sem=rs, device_id=to, device_id_type=MESH
        )

    def wcopy(j):
        return pltpu.make_async_copy(w_ref.at[:, WIDTH * j : WIDTH * (j + 1)], wbuf.at[j], wsem.at[j])

    for j in (1, 2, 0):
        wcopy(j).start()

    barrier = pltpu.get_barrier_semaphore()
    partners = [cp] + xd + [to for to, _ in yzd]
    for p in partners:
        pl.semaphore_signal(barrier, inc=1, device_id=p, device_id_type=MESH)

    half = BLK // 2
    top, bot = pl.ds(0, half), pl.ds(half, half)
    a0 = rcopy(hidden_ref.at[top], land.at[0, top], hs.at[0], hr.at[0], right)
    a1 = rcopy(hidden_ref.at[bot], land.at[1, bot], hs.at[1], hr.at[1], left)
    a2 = rcopy(hidden_ref.at[bot], land.at[0, bot], hs.at[2], hr.at[2], right)
    a3 = rcopy(hidden_ref.at[top], land.at[1, top], hs.at[3], hr.at[3], left)
    b0 = rcopy(land.at[0, top], land.at[2, top], hs.at[4], hr.at[4], right)
    b1 = rcopy(land.at[1, bot], land.at[2, bot], hs.at[5], hr.at[5], left)

    def slot(xb):
        return jnp.where(zh == 0, xb, 3 - xb)

    def turn(c):
        t = jnp.where(zh == 0, c, 7 - c)
        for h in range(NH):
            kvt[h, :, lanes(t * BLK, BLK)] = kv[c, h].T

    def kvcopy(c, xb):
        return rcopy(kv.at[c], kv.at[c], ks.at[xb], kr.at[xb], zp)

    def normalize(h):
        h = h.astype(F32)
        scale = lax.rsqrt(jnp.mean(h * h, axis=1, keepdims=True) + 1e-06)
        return (h * scale).astype(BF)

    def keep_turned(normed, xb):
        turned = normed.T
        for j in range(8):
            for par in range(2):
                at = 192 * j + 96 * par
                nt[par, 96 * j : 96 * (j + 1), lanes(xb * BLK, BLK)] = turned[at : at + 96, :]

    def arrive(xb):
        theirs = (1 - zh) * 4 + xb
        kvcopy(theirs, xb).wait_recv()
        turn(theirs)

    def group_copies(src, dst, ss, rs):
        return [rcopy(src.at[mod4(x + d)], dst, ss.at[i], rs.at[i], xd[i]) for i, d in enumerate(STEPS)]

    qz[...] = jnp.zeros_like(qz)
    uz[...] = jnp.zeros_like(uz)
    normed = normalize(hidden_ref[...])
    wcopy(1).wait()
    k = dot(normed, wbuf[1]).astype(BF)
    wcopy(2).wait()
    v = dot(normed, wbuf[2]).astype(BF)
    for g in range(4):
        for i in range(NH):
            cols = slice(GW * g + HS * i, GW * g + HS * (i + 1))
            kvsend[g, i] = jnp.concatenate([k[:, cols], v[:, cols]], axis=1)
    pl.semaphore_wait(barrier, len(partners))
    mine_c = zh * 4 + x
    kvx = group_copies(kvsend, kv.at[mine_c], as_, ar)
    for i in (1, 0, 2):
        kvx[i].start()
    kv[mine_c] = kvsend[x]
    kvcopy(mine_c, x).start()
    wcopy(0).wait()
    q = (dot(normed, wbuf[0]).astype(BF).astype(F32) * SCALE).T.astype(BF)
    for g in range(4):
        qsend[g] = q[GW * g : GW * (g + 1), :]
    qx = group_copies(qsend, qland.at[x], ps, pr)
    for i in (1, 0, 2):
        qx[i].start()
    qland[x] = qsend[x]
    keep = mask_ref[...] == 1
    for g in range(4):
        u = cot_ref[:, GW * g : GW * (g + 1)].astype(F32).T
        usend[g] = jnp.where(keep, u, 0.0).astype(BF)
    ux = group_copies(usend, ut.at[x], us, ur)
    for i in (1, 0, 2):
        ux[i].start()
    ut[x] = usend[x]
    keep_turned(normed, x)
    turn(mine_c)
    for i, d in ((0, 3), (2, 1), (1, 2)):
        kvx[i].wait_recv()
        xb = mod4(x + d)
        kvcopy(zh * 4 + xb, xb).start()
        turn(zh * 4 + xb)
    arrive(x)
    for c in qx:
        c.wait_recv()
    for c in (a0, a1, a2, a3):
        c.start()
    for xb in range(4):
        for i in range(NH):
            qz[i, 0:HS, lanes(slot(xb) * BLK, BLK)] = qland[xb, HS * i : HS * (i + 1), :]
    for c in ux:
        c.wait_recv()
    for xb in range(4):
        for i in range(NH):
            uz[i, HS : 2 * HS, lanes(slot(xb) * BLK, BLK)] = ut[xb, HS * i : HS * (i + 1), :]
    for c in kvx + qx + ux:
        c.wait_send()

    def zcopy(h, part):
        return rcopy(zsend.at[h, part], zland.at[h, part], zs.at[h, part], zr.at[h, part], zp)

    s1, r1, s5, r5, s3, r3 = (s1a, s1b), (r1a, r1b), (s5a, s5b), (r5a, r5b), (s3a, s3b), (r3a, r3b)

    def ccopy(n):
        return rcopy(s1[n], r1[n], cs.at[n], cr.at[n], cp)

    def ocopy(h, i):
        rows = pl.ds(pl.multiple_of(h * HS, HS), HS)
        return rcopy(osend.at[h, mod4(x + STEPS[i])], oland.at[x, rows], osm.at[h, i], orm.at[h, i], xd[i])

    def gather_grads(h):
        gbuf[h, 0:HS, :] = qg[h]
        for part in range(2):
            zcopy(h, part).wait()
            gbuf[h, HS * (part + 1) : HS * (part + 2), :] = (own[h, part] + zland[h, part].astype(F32)).astype(BF)

    def product(par, heads, blocks):
        total = None
        for xb in blocks:
            at_ = lanes(xb * BLK, BLK)
            g = jnp.concatenate([gbuf[h, :, at_] for h in heads], axis=0)
            p = dot_nt(nt[par, :, at_], g)
            total = p if total is None else total + p
        return total

    def dcopy(n, i):
        to, place = yzd[i]
        return rcopy(s5[n].at[place], r5[n].at[i], ds.at[n, i], dr.at[n, i], to)

    def to_yz(n, own_part):
        ccopy(n).wait()
        both = (own_part + r1[n][...].astype(F32)).astype(BF)
        for l in range(2):
            for yy in range(4):
                for u in range(2):
                    row = 384 * l + 96 * yy + 48 * u
                    s5[n][yy * 4 + 2 * u + l] = both[row : row + 48, :]
        for i in range(15):
            dcopy(n, i).start()

    def xcopy(n, i):
        return rcopy(s3[n].at[mod4(x + STEPS[i])], r3[n].at[x], xs.at[n, i], xr.at[n, i], xd[i])

    def to_x(n, width):
        t = s5[n][y * 4 + z].astype(F32)
        for i in range(15):
            dcopy(n, i).wait()
            t = t + r5[n][i].astype(F32)
        for xb in range(4):
            s3[n][xb, 0:12, 0:width] = t[12 * xb : 12 * (xb + 1), :]
        for i in range(3):
            xcopy(n, i).start()
        r3[n][x] = s3[n][x]

    e0 = len_ref[0, 0]
    e1 = e0 + len_ref[0, 1]

    def segment(pos):
        return (pos >= e0).astype(jnp.int32) + (pos >= e1).astype(jnp.int32)

    def key_block(t):
        return jnp.where(zh == 0, t, 7 - t)

    def slots(t):
        return range(max(0, t - 4), 4)

    def qpos(j):
        return zh * HALF + BLK * jnp.where(zh == 0, j, 3 - j)

    qsegs = [segment(qpos(j) + lax.broadcasted_iota(jnp.int32, (1, BLK), 1)) for j in range(4)]

    def at(j):
        return slice(BLK * j, BLK * (j + 1))

    def scores(h, steps):
        for t in steps:
            c = key_block(t)
            kseg = segment(c * BLK + lax.broadcasted_iota(jnp.int32, (BLK, 1), 0))
            for j in slots(t):
                s = dot(kv[c, h], qz[h, :, at(j)])
                s = jnp.where(kseg == qsegs[j], s, NEG)
                s_scr[at(t), at(j)] = s
                m = jnp.max(s, axis=0, keepdims=True)
                mx[0:1, at(j)] = m if t == 0 else jnp.maximum(mx[0:1, at(j)], m)

    def head(h, carry):
        scores(h, range(4, 8))

        ms = [mx[0:1, at(j)] for j in range(4)]
        ts = [jnp.zeros((1, BLK), F32) for _ in range(4)]
        for t in range(8):
            c = key_block(t)
            for j in slots(t):
                p = jnp.exp(s_scr[at(t), at(j)] - ms[j])
                ts[j] = ts[j] + jnp.sum(p, axis=0, keepdims=True)
                p_scr[at(t), at(j)] = p.astype(BF)
                s_scr[at(t), at(j)] = dot(kv[c, h], uz[h, :, at(j)])

        rts = [1.0 / ts[j] for j in range(4)]
        us_ = [uz[h, HS : 2 * HS, at(j)].astype(F32) for j in range(4)]
        urs = [(us_[j] * rts[j]).astype(BF) for j in range(4)]
        qrs = [(qz[h, 0:HS, at(j)].astype(F32) * rts[j]).astype(BF) for j in range(4)]

        def put(t, part, g):
            if t >= 4:
                zsend[h, part, :, lanes(jnp.where(zh == 0, t - 4, 7 - t) * BLK, BLK)] = g.astype(BF)
            else:
                own[h, part, :, lanes(jnp.where(zh == 0, t, 3 - t) * BLK, BLK)] = g

        def value_grad(t):
            g = jnp.zeros((HS, BLK), F32)
            for j in slots(t):
                g = g + dot_nt(urs[j], p_scr[at(t), at(j)])
            put(t, 1, g)

        def key_grad(t):
            g = jnp.zeros((HS, BLK), F32)
            for j in slots(t):
                ds_ = p_scr[at(t), at(j)].astype(F32) * (s_scr[at(t), at(j)] - deltas[j])
                ds_ = ds_.astype(BF)
                g_scr[at(t), at(j)] = ds_
                g = g + dot_nt(qrs[j], ds_)
            put(t, 0, g)

        for t in (7, 6, 5, 4):
            value_grad(t)
        zcopy(h, 1).start()

        deltas = []
        for j in range(4):
            rows = slice(0, BLK * (5 + j))
            o = (dot(kvt[h, HS : 2 * HS, rows], p_scr[rows, at(j)]) / ts[j]).astype(BF)
            osend[h, jnp.where(zh == 0, j, 3 - j)] = o
            deltas.append(jnp.sum(us_[j] * o.astype(F32), axis=0, keepdims=True))
        oland[x, pl.ds(pl.multiple_of(h * HS, HS), HS), :] = osend[h, x]

        for t in (7, 6, 5, 4):
            key_grad(t)
        zcopy(h, 0).start()

        for t in (3, 2, 1, 0):
            value_grad(t)
            key_grad(t)
        for j in range(4):
            rows = slice(0, BLK * (5 + j))
            g = dot(kvt[h, 0:HS, rows], g_scr[rows, at(j)]) * (rts[j] * SCALE)
            qg[h, :, lanes(jnp.where(zh == 0, j, 3 - j) * BLK, BLK)] = g.astype(BF)

        @pl.when(h == 0)
        def _():
            a0.wait_recv()
            b0.start()
            a1.wait_recv()
            b1.start()

        @pl.when(h == 1)
        def _():
            a2.wait_recv()
            keep_turned(normalize(land[0]), mod4(x + 3))
            a3.wait_recv()
            keep_turned(normalize(land[1]), mod4(x + 1))

        @pl.when(h < NH - 1)
        def _():
            scores(h + 1, range(4))

        return carry

    scores(0, range(4))
    for d in (3, 1, 2):
        arrive(mod4(x + d))
    for xb in range(4):
        kvcopy(zh * 4 + xb, xb).wait_send()
    lax.fori_loop(0, NH, head, 0)
    near, last = (x, mod4(x + 1), mod4(x + 3)), (mod4(x + 2),)
    gather_grads(0)
    gather_grads(1)
    theirs[...] = product(1 - core, (0, 1), near)
    mine[...] = product(core, (0, 1), near)
    b0.wait_recv()
    b1.wait_recv()
    keep_turned(normalize(land[2]), mod4(x + 2))
    s1a[...] = (theirs[...] + product(1 - core, (0, 1), last)).astype(BF)
    ccopy(0).start()
    for c in (a0, a1, a2, a3, b0, b1):
        c.wait_send()
    for h in range(NH):
        for i in range(3):
            ocopy(h, i).start()
    mine[...] += product(core, (0, 1), last)
    gather_grads(2)
    s1b[...] = product(1 - core, (2,), near + last).astype(BF)
    ccopy(1).start()
    to_yz(0, mine[...])
    to_yz(1, product(core, (2,), near + last))
    to_x(0, 2 * GW)
    to_x(1, GW)
    for h in range(NH):
        for i in range(3):
            ocopy(h, i).wait()
    for n in range(2):
        for i in range(3):
            xcopy(n, i).wait()


def main(lengths, hidden, mask, cot, w):
    dma = pltpu.SemaphoreType.DMA
    return pl.pallas_call(
        main_kernel,
        out_shape=(
            jax.ShapeDtypeStruct((4, GW, BLK), BF),
            jax.ShapeDtypeStruct((4, 16, 2 * GW), F32),
            jax.ShapeDtypeStruct((4, 16, 256), F32),
        ),
        in_specs=[pl.BlockSpec(memory_space=pltpu.SMEM)]
        + [pl.BlockSpec(memory_space=VMEM)] * 3
        + [pl.BlockSpec(memory_space=pl.ANY)],
        out_specs=[pl.BlockSpec(memory_space=VMEM)] * 3,
        scratch_shapes=[
            VMEM((3, BLK, D), BF),
            VMEM((3, D, WIDTH), BF),
            VMEM((4, GW, BLK), BF),
            VMEM((4, GW, BLK), BF),
            VMEM((4, NH, BLK, 2 * HS), BF),
            VMEM((8, NH, BLK, 2 * HS), BF),
            VMEM((NH, 2 * HS, 8 * BLK), BF),
            VMEM((4, GW, BLK), BF),
            VMEM((4, GW, BLK), BF),
            VMEM((NH, 2 * HS, HALF), BF),
            VMEM((NH, 2 * HS, HALF), BF),
            VMEM((2, WIDTH, HALF), BF),
            VMEM((8 * BLK, HALF), F32),
            VMEM((8 * BLK, HALF), BF),
            VMEM((8 * BLK, HALF), BF),
            VMEM((NH, HS, HALF), BF),
            VMEM((NH, 2, HS, HALF), F32),
            VMEM((NH, 2, HS, HALF), BF),
            VMEM((NH, 2, HS, HALF), BF),
            VMEM((NH, 4, HS, BLK), BF),
            VMEM((NH, GW, HALF), BF),
            VMEM((WIDTH, 2 * GW), F32),
            VMEM((WIDTH, 2 * GW), F32),
            VMEM((WIDTH, 2 * GW), BF),
            VMEM((WIDTH, 2 * GW), BF),
            VMEM((WIDTH, GW), BF),
            VMEM((WIDTH, GW), BF),
            VMEM((16, 48, 2 * GW), BF),
            VMEM((15, 48, 2 * GW), BF),
            VMEM((16, 48, GW), BF),
            VMEM((15, 48, GW), BF),
            VMEM((4, 16, 2 * GW), F32),
            VMEM((4, 16, 256), F32),
            VMEM((8, HALF), F32),
            dma((3,)), dma((6,)), dma((6,)), dma((3,)), dma((3,)), dma((3,)), dma((3,)),
            dma((4,)), dma((4,)), dma((3,)), dma((3,)),
            dma((NH, 2)), dma((NH, 2)), dma((NH, 3)), dma((NH, 3)), dma((2,)), dma((2,)),
            dma((2, 15)), dma((2, 15)), dma((2, 3)), dma((2, 3)),
        ],
        compiler_params=pltpu.CompilerParams(collective_id=0, has_side_effects=True, vmem_limit_bytes=LIMIT),
        name="main",
    )(lengths, hidden, mask, cot, w)


def lay_out_kernel(ot_ref, wa_ref, wb_ref, out_ref, wg_ref):
    for g in range(4):
        at = GW * g
        out_ref[:, at : at + GW] = ot_ref[g].astype(F32).T.astype(BF)
        for h in range(NH):
            for part in range(3):
                src = (GW * h if h < 2 else 0) + HS * part
                to = WIDTH * part + at + HS * h
                wg_ref[:, to : to + HS] = (wa_ref if h < 2 else wb_ref)[g, 0:12, src : src + HS]


def lay_out(ot, wa, wb):
    return pl.pallas_call(
        lay_out_kernel,
        out_shape=(
            jax.ShapeDtypeStruct((BLK, WIDTH), BF),
            jax.ShapeDtypeStruct((12, 3 * WIDTH), F32),
        ),
        in_specs=[pl.BlockSpec(memory_space=VMEM)] * 3,
        out_specs=[pl.BlockSpec(memory_space=VMEM)] * 2,
        name="lay_out",
    )(ot, wa, wb)


def shards(hidden, masked, clip_lengths, qkv_weight, cotangent):
    return lay_out(*main(clip_lengths, hidden, masked.reshape(1, BLK), cotangent, qkv_weight))


def solution(mesh):
    in_specs = (
        P(("dp", "seq"), None),
        P(("dp", "seq")),
        P("dp", None),
        P(),
        P(("dp", "seq"), None),
    )
    out_specs = (P(("dp", "seq"), None), P(("dp", "seq"), None))
    return jax.shard_map(shards, mesh=mesh, in_specs=in_specs, out_specs=out_specs, check_vma=False)
```

time: 90.4 us -> 83.4 us (0.923)
  Pallas kernels: 89.6 us -> 82.6 us
    pallas_call x1, Pallas kernels: 87.5 us -> 80.4 us  [main(): pl.pallas_call(main_kernel, out_shape=(jax.ShapeDtypeStruct((4, GW, BLK),...]
where the time goes in v4:
time: 83.4 us; the launch traced here: 83.2 us
  Pallas kernels  82.6 us (99%)
    pallas_call x1, Pallas kernels, main(): pl.pallas_call(main_kernel, out_shape=(jax.ShapeDtypeStruct((4, GW, BLK),...  80.4 us
    pallas_call x1, Pallas kernels, lay_out(): pl.pallas_call(lay_out_kernel, out_shape=(jax.ShapeDtypeStruct((BLK, WIDT...  2.16 us

profile of v4, /device:TPU:0, one launch (start us, length us, event | category | flops | bytes accessed | tf_op | source)
XLA Modules:
  0.0 83.2 jit_solution(3939301473113918079)
XLA Ops:
  0.6 80.4 %main.1 = (bf16[4,192,256]{2,1,0:T(8,128)(2,1)}, f32[4,16,384]{2,1,0:T(8,128)}, f32[4,16,256]{2,1,0:T(8,128)}) custom-call(s32[1,3]{1,0:T(1,128)} %len_ref.1, bf16[256,1536]{1,0:T(8,128)(2,1)} %hidden_ref.1, s32[1,256]{1,0:T(1,128)} %bitcast.1, bf16[256,768]{1,0:T(8,128)(2,1)} %cot_ref.1, bf16[1536,2304]{1,0:T(8,128)(2,1)} %w_ref.1), custom_call_target="tpu_custom_call" | custom-call | tf_op jit(solution)/shard_map/main/pallas_call | solution.py:393
  81.1 2.2 %lay_out.1 = (bf16[256,768]{1,0:T(8,128)(2,1)}, f32[12,2304]{1,0:T(8,128)}) custom-call(bf16[4,192,256]{2,1,0:T(8,128)(2,1)} %get-tuple-element.5.ot_ref, f32[4,16,384]{2,1,0:T(8,128)} %get-tuple-element.6.wa_ref, f32[4,16,256]{2,1,0:T(8,128)} %get-tuple-element.7.wb_ref), custom_call_target="tpu_custom_call" | custom-call | tf_op jit(solution)/shard_map/lay_out/pallas_call | solution.py:461

commit v5 on v4

--- a/solution.py
+++ b/solution.py
@@ -44,8 +44,8 @@
     len_ref, hidden_ref, mask_ref, cot_ref, w_ref,
     oland, r3a, r3b,
     land, wbuf, usend, ut, kvsend, kv, kvt, qsend, qland, qz, uz, nt, s_scr, p_scr, g_scr,
-    qg, own, zsend, zland, osend, gbuf, theirs, mine, s1a, r1a, s1b, r1b, s5a, r5a, s5b, r5b, s3a, s3b, mx,
-    wsem, hs, hr, as_, ar, ps, pr, ks, kr, us, ur, zs, zr, osm, orm, cs, cr, ds, dr, xs, xr,
+    qg, own, zsend, zland, osend, gbuf, theirs, mine, s1a, r1a, s1b, r1b, s2y, r2y, s4y, r4y, s2z, r2z, s4z, r4z, s5, r5, s3a, s3b, mx,
+    wsem, hs, hr, as_, ar, ps, pr, ks, kr, us, ur, zs, zr, osm, orm, cs, cr, ts_, tr_, ds, dr, xs, xr,
 ):
     dp = lax.axis_index("dp")
     sq = lax.axis_index("seq")
@@ -173,18 +173,11 @@
     for xb in range(4):
         for i in range(NH):
             qz[i, 0:HS, lanes(slot(xb) * BLK, BLK)] = qland[xb, HS * i : HS * (i + 1), :]
-    for c in ux:
-        c.wait_recv()
-    for xb in range(4):
-        for i in range(NH):
-            uz[i, HS : 2 * HS, lanes(slot(xb) * BLK, BLK)] = ut[xb, HS * i : HS * (i + 1), :]
-    for c in kvx + qx + ux:
-        c.wait_send()
 
     def zcopy(h, part):
         return rcopy(zsend.at[h, part], zland.at[h, part], zs.at[h, part], zr.at[h, part], zp)
 
-    s1, r1, s5, r5, s3, r3 = (s1a, s1b), (r1a, r1b), (s5a, s5b), (r5a, r5b), (s3a, s3b), (r3a, r3b)
+    s1, r1, s3, r3 = (s1a, s1b), (r1a, r1b), (s3a, s3b), (r3a, r3b)
 
     def ccopy(n):
         return rcopy(s1[n], r1[n], cs.at[n], cr.at[n], cp)
@@ -208,31 +201,65 @@
             total = p if total is None else total + p
         return total
 
-    def dcopy(n, i):
-        to, place = yzd[i]
-        return rcopy(s5[n].at[place], r5[n].at[i], ds.at[n, i], dr.at[n, i], to)
-
-    def to_yz(n, own_part):
-        ccopy(n).wait()
-        both = (own_part + r1[n][...].astype(F32)).astype(BF)
+    def stage(n, i):
+        to = (yd, zd, zd, yd)[n][i]
+        me = (y, z, z, y)[n]
+        src, dst = ((s2y, r2y), (s2z, r2z), (s4y, r4y), (s4z, r4z))[n]
+        return rcopy(src.at[mod4(me + STEPS[i])], dst.at[i], ts_.at[n, i], tr_.at[n, i], to)
+
+    def places():
         for l in range(2):
             for yy in range(4):
                 for u in range(2):
                     row = 384 * l + 96 * yy + 48 * u
-                    s5[n][yy * 4 + 2 * u + l] = both[row : row + 48, :]
+                    yield yy, 2 * u + l, slice(row, row + 48)
+
+    def first_stage():
+        ccopy(0).wait()
+        both = (mine[...] + r1a[...].astype(F32)).astype(BF)
+        for yy, zz, rows in places():
+            s2y[yy, zz] = both[rows, 0:256]
+        for i in range(3):
+            stage(0, i).start()
+        for yy, zz, rows in places():
+            s2z[zz, yy] = both[rows, 256 : 2 * GW]
+        for i in range(3):
+            stage(1, i).start()
+
+    def stage_sum(n, src, dst, at_):
+        t = src[at_].astype(F32)
+        for i in range(3):
+            stage(n, i).wait()
+            t = t + dst[i].astype(F32)
+        return t
+
+    def second_stage():
+        s4y[...] = stage_sum(0, s2y, r2y, y).astype(BF)
+        for i in range(3):
+            stage(2, i).start()
+        s4z[...] = stage_sum(1, s2z, r2z, z).astype(BF)
+        for i in range(3):
+            stage(3, i).start()
+
+    def dcopy(i):
+        to, place = yzd[i]
+        return rcopy(s5.at[place], r5.at[i], ds.at[i], dr.at[i], to)
+
+    def to_yz(own_part):
+        ccopy(1).wait()
+        both = (own_part + r1b[...].astype(F32)).astype(BF)
+        for yy, zz, rows in places():
+            s5[yy * 4 + zz] = both[rows, :]
         for i in range(15):
-            dcopy(n, i).start()
+            dcopy(i).start()
 
     def xcopy(n, i):
         return rcopy(s3[n].at[mod4(x + STEPS[i])], r3[n].at[x], xs.at[n, i], xr.at[n, i], xd[i])
 
-    def to_x(n, width):
-        t = s5[n][y * 4 + z].astype(F32)
-        for i in range(15):
-            dcopy(n, i).wait()
-            t = t + r5[n][i].astype(F32)
+    def to_x(n, columns):
         for xb in range(4):
-            s3[n][xb, 0:12, 0:width] = t[12 * xb : 12 * (xb + 1), :]
+            for t, first in columns:
+                s3[n][xb, 0:12, first : first + t.shape[1]] = t[12 * xb : 12 * (xb + 1), :]
         for i in range(3):
             xcopy(n, i).start()
         r3[n][x] = s3[n][x]
@@ -352,10 +379,17 @@
         return carry
 
     scores(0, range(4))
+    for c in ux:
+        c.wait_recv()
+    for xb in range(4):
+        for i in range(NH):
+            uz[i, HS : 2 * HS, lanes(slot(xb) * BLK, BLK)] = ut[xb, HS * i : HS * (i + 1), :]
     for d in (3, 1, 2):
         arrive(mod4(x + d))
     for xb in range(4):
         kvcopy(zh * 4 + xb, xb).wait_send()
+    for c in kvx + qx + ux:
+        c.wait_send()
     lax.fori_loop(0, NH, head, 0)
     near, last = (x, mod4(x + 1), mod4(x + 3)), (mod4(x + 2),)
     gather_grads(0)
@@ -376,10 +410,15 @@
     gather_grads(2)
     s1b[...] = product(1 - core, (2,), near + last).astype(BF)
     ccopy(1).start()
-    to_yz(0, mine[...])
-    to_yz(1, product(core, (2,), near + last))
-    to_x(0, 2 * GW)
-    to_x(1, GW)
+    first_stage()
+    to_yz(product(core, (2,), near + last))
+    second_stage()
+    to_x(0, [(stage_sum(2, s4y, r4y, z), 0), (stage_sum(3, s4z, r4z, y), 256)])
+    t = s5[y * 4 + z].astype(F32)
+    for i in range(15):
+        dcopy(i).wait()
+        t = t + r5[i].astype(F32)
+    to_x(1, [(t, 0)])
     for h in range(NH):
         for i in range(3):
             ocopy(h, i).wait()
@@ -429,8 +468,14 @@
             VMEM((WIDTH, 2 * GW), BF),
             VMEM((WIDTH, GW), BF),
             VMEM((WIDTH, GW), BF),
-            VMEM((16, 48, 2 * GW), BF),
-            VMEM((15, 48, 2 * GW), BF),
+            VMEM((4, 4, 48, 256), BF),
+            VMEM((3, 4, 48, 256), BF),
+            VMEM((4, 48, 256), BF),
+            VMEM((3, 48, 256), BF),
+            VMEM((4, 4, 48, 128), BF),
+            VMEM((3, 4, 48, 128), BF),
+            VMEM((4, 48, 128), BF),
+            VMEM((3, 48, 128), BF),
             VMEM((16, 48, GW), BF),
             VMEM((15, 48, GW), BF),
             VMEM((4, 16, 2 * GW), F32),
@@ -439,7 +484,7 @@
             dma((3,)), dma((6,)), dma((6,)), dma((3,)), dma((3,)), dma((3,)), dma((3,)),
             dma((4,)), dma((4,)), dma((3,)), dma((3,)),
             dma((NH, 2)), dma((NH, 2)), dma((NH, 3)), dma((NH, 3)), dma((2,)), dma((2,)),
-            dma((2, 15)), dma((2, 15)), dma((2, 3)), dma((2, 3)),
+            dma((4, 3)), dma((4, 3)), dma((15,)), dma((15,)), dma((2, 3)), dma((2, 3)),
         ],
         compiler_params=pltpu.CompilerParams(collective_id=0, has_side_effects=True, vmem_limit_bytes=LIMIT),
         name="main",

time: 83.4 us -> 81.9 us (0.982)
  Pallas kernels: 82.6 us -> 81.1 us
    pallas_call x1, Pallas kernels: 80.4 us -> 78.9 us  [main(): pl.pallas_call(main_kernel, out_shape=(jax.ShapeDtypeStruct((4, GW, BLK),...]
where the time goes in v5:
time: 81.9 us; the launch traced here: 81.7 us
  Pallas kernels  81.1 us (99%)
    pallas_call x1, Pallas kernels, main(): pl.pallas_call(main_kernel, out_shape=(jax.ShapeDtypeStruct((4, GW, BLK),...  78.9 us
    pallas_call x1, Pallas kernels, lay_out(): pl.pallas_call(lay_out_kernel, out_shape=(jax.ShapeDtypeStruct((BLK, WIDT...  2.16 us

profile of v5, /device:TPU:0, one launch (start us, length us, event | category | flops | bytes accessed | tf_op | source)
XLA Modules:
  0.0 81.7 jit_solution(6170432549453254185)
XLA Ops:
  0.6 78.9 %main.1 = (bf16[4,192,256]{2,1,0:T(8,128)(2,1)}, f32[4,16,384]{2,1,0:T(8,128)}, f32[4,16,256]{2,1,0:T(8,128)}) custom-call(s32[1,3]{1,0:T(1,128)} %len_ref.1, bf16[256,1536]{1,0:T(8,128)(2,1)} %hidden_ref.1, s32[1,256]{1,0:T(1,128)} %bitcast.1, bf16[256,768]{1,0:T(8,128)(2,1)} %cot_ref.1, bf16[1536,2304]{1,0:T(8,128)(2,1)} %w_ref.1), custom_call_target="tpu_custom_call" | custom-call | tf_op jit(solution)/shard_map/main/pallas_call | solution.py:432
  79.6 2.2 %lay_out.1 = (bf16[256,768]{1,0:T(8,128)(2,1)}, f32[12,2304]{1,0:T(8,128)}) custom-call(bf16[4,192,256]{2,1,0:T(8,128)(2,1)} %get-tuple-element.5.ot_ref, f32[4,16,384]{2,1,0:T(8,128)} %get-tuple-element.6.wa_ref, f32[4,16,256]{2,1,0:T(8,128)} %get-tuple-element.7.wb_ref), custom_call_target="tpu_custom_call" | custom-call | tf_op jit(solution)/shard_map/lay_out/pallas_call | solution.py:506

commit v6 on v5

--- a/solution.py
+++ b/solution.py
@@ -14,6 +14,8 @@
 HS = 64
 NH = 3
 GW = NH * HS
+CA = 2 * GW + HS
+CB = 2 * HS
 BLK = 256
 HALF = 4 * BLK
 D = 1536
@@ -192,11 +194,14 @@
             zcopy(h, part).wait()
             gbuf[h, HS * (part + 1) : HS * (part + 2), :] = (own[h, part] + zland[h, part].astype(F32)).astype(BF)
 
-    def product(par, heads, blocks):
+    def product(par, n, blocks):
         total = None
         for xb in blocks:
             at_ = lanes(xb * BLK, BLK)
-            g = jnp.concatenate([gbuf[h, :, at_] for h in heads], axis=0)
+            if n == 0:
+                g = jnp.concatenate([gbuf[0, :, at_], gbuf[1, :, at_], qg[2, :, at_]], axis=0)
+            else:
+                g = gbuf[2, HS:GW, at_]
             p = dot_nt(nt[par, :, at_], g)
             total = p if total is None else total + p
         return total
@@ -222,7 +227,7 @@
         for i in range(3):
             stage(0, i).start()
         for yy, zz, rows in places():
-            s2z[zz, yy] = both[rows, 256 : 2 * GW]
+            s2z[zz, yy] = both[rows, 256:CA]
         for i in range(3):
             stage(1, i).start()
 
@@ -394,24 +399,24 @@
     near, last = (x, mod4(x + 1), mod4(x + 3)), (mod4(x + 2),)
     gather_grads(0)
     gather_grads(1)
-    theirs[...] = product(1 - core, (0, 1), near)
-    mine[...] = product(core, (0, 1), near)
+    theirs[...] = product(1 - core, 0, near)
+    mine[...] = product(core, 0, near)
     b0.wait_recv()
     b1.wait_recv()
     keep_turned(normalize(land[2]), mod4(x + 2))
-    s1a[...] = (theirs[...] + product(1 - core, (0, 1), last)).astype(BF)
+    s1a[...] = (theirs[...] + product(1 - core, 0, last)).astype(BF)
     ccopy(0).start()
     for c in (a0, a1, a2, a3, b0, b1):
         c.wait_send()
     for h in range(NH):
         for i in range(3):
             ocopy(h, i).start()
-    mine[...] += product(core, (0, 1), last)
+    mine[...] += product(core, 0, last)
+    first_stage()
     gather_grads(2)
-    s1b[...] = product(1 - core, (2,), near + last).astype(BF)
+    s1b[...] = product(1 - core, 1, near + last).astype(BF)
     ccopy(1).start()
-    first_stage()
-    to_yz(product(core, (2,), near + last))
+    to_yz(product(core, 1, near + last))
     second_stage()
     to_x(0, [(stage_sum(2, s4y, r4y, z), 0), (stage_sum(3, s4z, r4z, y), 256)])
     t = s5[y * 4 + z].astype(F32)
@@ -433,8 +438,8 @@
         main_kernel,
         out_shape=(
             jax.ShapeDtypeStruct((4, GW, BLK), BF),
-            jax.ShapeDtypeStruct((4, 16, 2 * GW), F32),
-            jax.ShapeDtypeStruct((4, 16, 256), F32),
+            jax.ShapeDtypeStruct((4, 16, CA), F32),
+            jax.ShapeDtypeStruct((4, 16, CB), F32),
         ),
         in_specs=[pl.BlockSpec(memory_space=pltpu.SMEM)]
         + [pl.BlockSpec(memory_space=VMEM)] * 3
@@ -462,24 +467,24 @@
             VMEM((NH, 2, HS, HALF), BF),
             VMEM((NH, 4, HS, BLK), BF),
             VMEM((NH, GW, HALF), BF),
-            VMEM((WIDTH, 2 * GW), F32),
-            VMEM((WIDTH, 2 * GW), F32),
-            VMEM((WIDTH, 2 * GW), BF),
-            VMEM((WIDTH, 2 * GW), BF),
-            VMEM((WIDTH, GW), BF),
-            VMEM((WIDTH, GW), BF),
+            VMEM((WIDTH, CA), F32),
+            VMEM((WIDTH, CA), F32),
+            VMEM((WIDTH, CA), BF),
+            VMEM((WIDTH, CA), BF),
+            VMEM((WIDTH, CB), BF),
+            VMEM((WIDTH, CB), BF),
             VMEM((4, 4, 48, 256), BF),
             VMEM((3, 4, 48, 256), BF),
             VMEM((4, 48, 256), BF),
             VMEM((3, 48, 256), BF),
-            VMEM((4, 4, 48, 128), BF),
-            VMEM((3, 4, 48, 128), BF),
-            VMEM((4, 48, 128), BF),
-            VMEM((3, 48, 128), BF),
-            VMEM((16, 48, GW), BF),
-            VMEM((15, 48, GW), BF),
-            VMEM((4, 16, 2 * GW), F32),
-            VMEM((4, 16, 256), F32),
+            VMEM((4, 4, 48, CA - 256), BF),
+            VMEM((3, 4, 48, CA - 256), BF),
+            VMEM((4, 48, CA - 256), BF),
+            VMEM((3, 48, CA - 256), BF),
+            VMEM((16, 48, CB), BF),
+            VMEM((15, 48, CB), BF),
+            VMEM((4, 16, CA), F32),
+            VMEM((4, 16, CB), F32),
             VMEM((8, HALF), F32),
             dma((3,)), dma((6,)), dma((6,)), dma((3,)), dma((3,)), dma((3,)), dma((3,)),
             dma((4,)), dma((4,)), dma((3,)), dma((3,)),
@@ -497,9 +502,12 @@
         out_ref[:, at : at + GW] = ot_ref[g].astype(F32).T.astype(BF)
         for h in range(NH):
             for part in range(3):
-                src = (GW * h if h < 2 else 0) + HS * part
+                src = GW * h + HS * part
                 to = WIDTH * part + at + HS * h
-                wg_ref[:, to : to + HS] = (wa_ref if h < 2 else wb_ref)[g, 0:12, src : src + HS]
+                if src < CA:
+                    wg_ref[:, to : to + HS] = wa_ref[g, 0:12, src : src + HS]
+                else:
+                    wg_ref[:, to : to + HS] = wb_ref[g, 0:12, src - CA : src - CA + HS]
 
 
 def lay_out(ot, wa, wb):

time: 81.9 us -> 81.3 us (level)
  no operation moved by 1% of the time
where the time goes in v6:
time: 81.3 us; the launch traced here: 81.2 us
  Pallas kernels  80.6 us (99%)
    pallas_call x1, Pallas kernels, main(): pl.pallas_call(main_kernel, out_shape=(jax.ShapeDtypeStruct((4, GW, BLK),...  78.4 us
    pallas_call x1, Pallas kernels, lay_out(): pl.pallas_call(lay_out_kernel, out_shape=(jax.ShapeDtypeStruct((BLK, WIDT...  2.18 us

profile of v6, /device:TPU:0, one launch (start us, length us, event | category | flops | bytes accessed | tf_op | source)
XLA Modules:
  0.0 81.2 jit_solution(13831538868561143626)
XLA Ops:
  0.6 78.4 %main.1 = (bf16[4,192,256]{2,1,0:T(8,128)(2,1)}, f32[4,16,448]{2,1,0:T(8,128)}, f32[4,16,128]{2,1,0:T(8,128)}) custom-call(s32[1,3]{1,0:T(1,128)} %len_ref.1, bf16[256,1536]{1,0:T(8,128)(2,1)} %hidden_ref.1, s32[1,256]{1,0:T(1,128)} %bitcast.1, bf16[256,768]{1,0:T(8,128)(2,1)} %cot_ref.1, bf16[1536,2304]{1,0:T(8,128)(2,1)} %w_ref.1), custom_call_target="tpu_custom_call" | custom-call | tf_op jit(solution)/shard_map/main/pallas_call | solution.py:437
  79.0 2.2 %lay_out.1 = (bf16[256,768]{1,0:T(8,128)(2,1)}, f32[12,2304]{1,0:T(8,128)}) custom-call(bf16[4,192,256]{2,1,0:T(8,128)(2,1)} %get-tuple-element.5.ot_ref, f32[4,16,448]{2,1,0:T(8,128)} %get-tuple-element.6.wa_ref, f32[4,16,128]{2,1,0:T(8,128)} %get-tuple-element.7.wb_ref), custom_call_target="tpu_custom_call" | custom-call | tf_op jit(solution)/shard_map/lay_out/pallas_call | solution.py:514
